TPU v7x, 256 devices: a whole 4x4x8 slice. The times are simulated.
256 devices in a mesh: gx: 16 (over z, core), gy: 4 (over y), gz: 4 (over x).
Axes of the slice: x: 4, y: 4, z: 8, core: 2. Of those that a mesh axis runs over, the one named last changes fastest.
Arguments:
- fields: bfloat16 [6, 128, 512, 512], P(None, 'gz', 'gx', 'gy'), may hold values from -140 to 140, as said below
- phase_mask: int32 [128, 512, 512], P('gz', 'gx', 'gy'), may hold values 0 or 1
- w_first: float32 [3, 3, 3, 7, 32], replicated, may hold values from -0.4375 to 0.4375
- w_second: float32 [3, 3, 3, 32, 32], replicated, may hold values from -0.21875 to 0.21875
- w_third: float32 [3, 3, 3, 32, 32], replicated, may hold values from -0.21875 to 0.21875
- w_last: float32 [3, 3, 3, 32, 1], replicated, may hold values from -0.21875 to 0.21875
Outputs:
- prediction: float32 [16, 64, 64], P('gz', 'gx', 'gy')
- target: float32 [16, 64, 64], P('gz', 'gx', 'gy')
- grad_first: float32 [3, 3, 3, 7, 32], replicated
- grad_second: float32 [3, 3, 3, 32, 32], replicated
- grad_third: float32 [3, 3, 3, 32, 32], replicated
- grad_last: float32 [3, 3, 3, 32, 1], replicated
Inputs may be any that keep to these rules, and one draw needn't show every extreme that they name: fields[0] lies between 0 and 1.
All inputs are finite; a program needn't handle non-finite values. No bound on the sum of `phase_mask` on one device may be relied on, other than what follows from the above.
Results may differ from a plain program's by a relative error of at most 0.0003.
The roundings to bfloat16 on the way count: a program that leaves them out, or rounds other values in their place, can miss the bound.
Values may be sent and summed in bfloat16 or wider, within the bound.
A program may use at most 192 MiB of HBM per device.

v0:
```python
import jax
import jax.numpy as jnp
import numpy as np
from jax import lax
from jax.sharding import PartitionSpec as P

tap_offsets = np.arange(16) - 7.5
tap_raw = np.exp(-6.0 * tap_offsets * tap_offsets / 64.0)
filter_taps = tap_raw / tap_raw.sum()


def with_halo(array, sides, width):
    for axis, dim in sides:
        count, length = (lax.axis_size(axis), array.shape[dim])
        up = [(i, (i + 1) % count) for i in range(count - 1)]
        down = [(j, i) for i, j in up]
        last = lax.slice_in_dim(array, length - width, length, axis=dim)
        initial = lax.slice_in_dim(array, 0, width, axis=dim)
        before = lax.ppermute(last, axis, up)
        after = lax.ppermute(initial, axis, down)
        array = jnp.concatenate([before, array, after], axis=dim)
    return array


def reduce_axis(padded, along_dim):
    in_shape = padded.shape
    blocks = padded.reshape(
        in_shape[:along_dim] + (in_shape[along_dim] // 8, 8) + in_shape[along_dim + 1 :]
    )
    tap_values = jnp.asarray(filter_taps, dtype=jnp.float32)
    tap_shape = [1] * blocks.ndim
    tap_shape[along_dim + 1] = 8
    block_count = blocks.shape[along_dim]
    lower_half = lax.slice_in_dim(blocks, 0, block_count - 1, axis=along_dim) * tap_values[
        :8
    ].reshape(tuple(tap_shape))
    upper_half = lax.slice_in_dim(blocks, 1, block_count, axis=along_dim) * tap_values[8:].reshape(
        tuple(tap_shape)
    )
    return jnp.sum(lower_half, axis=along_dim + 1) + jnp.sum(upper_half, axis=along_dim + 1)


def valid_conv(volume, kernel):
    return lax.conv_general_dilated(
        volume[None],
        kernel,
        (1, 1, 1),
        "VALID",
        dimension_numbers=("NDHWC", "DHWIO", "NDHWC"),
        precision=lax.Precision.HIGHEST,
    )[0]


def flipped(kernel):
    return jnp.swapaxes(kernel[::-1, ::-1, ::-1], 3, 4)


def silu_slope(preact):
    sigma = jax.nn.sigmoid(preact)
    return sigma * (1.0 + preact * (1.0 - sigma))


def kernel_grad(padded_in, kernel, cotangent):

    def apply_kernel(current):
        return valid_conv(padded_in, current)

    unused_value, pullback = jax.vjp(apply_kernel, kernel)
    return pullback(cotangent)[0]


def bordered(volume):
    return with_halo(volume, (("gx", 1), ("gy", 2), ("gz", 0)), 1)


def shards(fields, phase_mask, w_first, w_second, w_third, w_last):
    liquid = fields[0].astype(jnp.float32)
    superheat = fields[1].astype(jnp.float32)
    active = phase_mask.astype(jnp.float32) * liquid
    source = (active * superheat).astype(jnp.bfloat16)
    stacked = jnp.concatenate([fields, active.astype(jnp.bfloat16)[None], source[None]], axis=0)
    margined = with_halo(stacked, (("gx", 2), ("gy", 3), ("gz", 1)), 4)
    filtered = reduce_axis(margined.astype(jnp.float32), 3)
    filtered = reduce_axis(filtered, 2)
    filtered = reduce_axis(filtered, 1)
    subgrid = filtered[7] - filtered[6] * filtered[1]
    squares = jnp.concatenate(
        [jnp.sum(filtered[:7] * filtered[:7], axis=(1, 2, 3)), jnp.sum(subgrid * subgrid)[None]]
    )
    totals = lax.psum(squares, ("gx", "gy", "gz"))
    depth_cells, across_cells, along_cells = subgrid.shape
    cell_count = (
        depth_cells
        * across_cells
        * along_cells
        * lax.axis_size("gx")
        * lax.axis_size("gy")
        * lax.axis_size("gz")
    )
    scales = lax.rsqrt(totals / cell_count + 1e-06)
    inputs = jnp.transpose(filtered[:7], (1, 2, 3, 0)) * scales[:7]
    target = subgrid * scales[7]
    weights = (w_first, w_second, w_third, w_last)
    saved_inputs = []
    saved_preacts = []
    activation = inputs
    for layer_index in range(len(weights)):
        padded_act = bordered(activation)
        preact = valid_conv(padded_act, weights[layer_index])
        saved_inputs.append(padded_act)
        saved_preacts.append(preact)
        activation = jax.nn.silu(preact) if layer_index < len(weights) - 1 else preact
    predicted = activation[..., 0]
    cotangent = 2.0 / cell_count * (predicted - target)[..., None]
    gradients = [w_first, w_second, w_third, w_last]
    for layer_index in range(len(weights) - 1, -1, -1):
        gradients[layer_index] = kernel_grad(
            saved_inputs[layer_index], weights[layer_index], cotangent
        )
        if layer_index > 0:
            back_flow = valid_conv(bordered(cotangent), flipped(weights[layer_index]))
            cotangent = back_flow * silu_slope(saved_preacts[layer_index - 1])
    summed = lax.psum((gradients[0], gradients[1], gradients[2], gradients[3]), ("gx", "gy", "gz"))
    return (predicted, target, summed[0], summed[1], summed[2], summed[3])


def solution(mesh):
    in_specs = (P(None, "gz", "gx", "gy"), P("gz", "gx", "gy"), P(), P(), P(), P())
    out_specs = (P("gz", "gx", "gy"), P("gz", "gx", "gy"), P(), P(), P(), P())
    return jax.shard_map(shards, mesh=mesh, in_specs=in_specs, out_specs=out_specs, check_vma=False)
```

profile of v0, /device:TPU:1, one launch (start us, length us, event | category | flops | bytes accessed | tf_op | source)
XLA Modules:
  0.0 700.9 jit_solution(5849562193523091195)
XLA Ops:
  10.6 4.9 collective-permute-start
  18.2 5.8 copy.375
  24.0 6.1 copy.374
  30.1 6.1 copy.376
  47.3 4.1 collective-permute-done.3
  51.4 16.2 %pad_maximum_fusion = bf16[8,32,40,136]{2,3,1,0:T(8,128)(2,1)S(1)} fusion(bf16[8,32,40,4]{2,3,1,0:T(4,128)(2,1)S(1)} %collective-permute-done.3, bf16[8,32,4,128]{2,3,1,0:T(8,128)(2,1)S(1)} %copy-done.2, bf16[8,32,32,128]{2,3,1,0:T(8,128)(2,1)} %copy.375, bf16[8,32,4,128]{2,3,1,0:T(8,128)(2,1)S(1)} %copy-done.1, ...), kind=kLoop, calls=%fused_computation.5 | loop fusion | flops 13926400 | bytes 5570560 | tf_op jit(solution)/shard_map/concatenate | solution.py:21
  75.3 18.6 %fusion.177 = bf16[8,32,40,17,8]{2,4,3,1,0:T(8,128)(2,1)} fusion(bf16[8,32,40,4]{2,3,1,0:T(4,128)(2,1)S(1)} %collective-permute-done.3, bf16[8,32,4,128]{2,3,1,0:T(8,128)(2,1)} %copy.376, bf16[8,32,32,128]{2,3,1,0:T(8,128)(2,1)} %copy.375, bf16[8,32,4,128]{2,3,1,0:T(8,128)(2,1)} %copy.374, bf16[8,32,40,4]{2,3,1,0:T(4,128)(2,1)S(1)} %collective-permute-done.2), kind=kLoop, calls=%fused_computation.269 | loop fusion | flops 13926400 | bytes 5570560 | tf_op jit(solution)/shard_map/concatenate | solution.py:21
  96.3 13.6 %maximum_convert_fusion = f32[8,40,40,17,8]{2,4,3,1,0:T(8,128)} fusion(bf16[8,4,40,17,8]{2,4,3,1,0:T(8,128)(2,1)S(1)} %bitcast.172, bf16[8,32,40,17,8]{2,4,3,1,0:T(8,128)(2,1)} %fusion.177, bf16[8,4,40,17,8]{2,4,3,1,0:T(8,128)(2,1)S(1)} %bitcast.171), kind=kLoop, calls=%fused_computation.4 | loop fusion | flops 5222400 | bytes 10444800 | tf_op jit(solution)/shard_map/convert_element_type | solution.py:83
  109.9 19.1 %fusion = (f32[8,40,40,16]{2,3,1,0:T(8,128)S(1)}, f32[8,40,40,16]{2,3,1,0:T(8,128)S(1)}) fusion(f32[8,40,40,17,8]{2,4,3,1,0:T(8,128)} %maximum_convert_fusion, f32[8]{0:T(128)S(1)} %copy-done.21, f32[8]{0:T(128)S(1)} %copy-done.20), kind=kLoop, calls=%fused_computation.1 | loop fusion | flops 6144000 | bytes 14745664 | tf_op jit(solution)/shard_map/reduce_sum | solution.py:40
  136.6 81.7 %psum.35 = f32[8]{0:T(128)S(1)} all-reduce(f32[8]{0:T(128)S(1)} %pad_maximum_fusion.58), channel_id=1, replica_groups=mesh['gx'=16,'gy'=4,'gz'=4] {'gx','gy','gz'}, use_global_device_ids=true, to_apply=%region_8.0 | all-reduce | flops 8 | bytes 64 | tf_op jit(solution)/shard_map/psum | solution.py:90
  245.0 4.5 collective-permute-start.12
  327.0 5.7 convolution_select_fusion.1
  335.2 3.8 collective-permute-start.30
  359.9 4.8 collective-permute-start.36
  379.4 8.0 %fusion.167 = f32[3,3,3,32,1]{3,4,2,1,0:T(1,128)S(1)} fusion(f32[1,6,6,18,32]{4,0,3,2,1:T(1,128)S(1)} %broadcast_in_dim.46, f32[1,4,4,16,1]{0,4,3,2,1:T(1,128)S(1)} %copy.430), kind=kOutput, calls=%fused_computation.268 | convolution fusion | flops 2654208 | bytes 87424 | tf_op jit(solution)/shard_map/transpose(jvp())/conv_general_dilated | solution.py:44
  387.7 4.5 convolution_select_fusion.3
  392.4 4.3 collective-permute-start.42
  405.0 9.3 %fusion.22 = f32[3,3,3,32,32]{4,3,2,1,0:T(8,128)} fusion(f32[6,6,8,3,32,1]{4,2,5,3,1,0:T(8,128)S(1)} %fusion.61, f32[6,6,8,3,32,1]{4,2,5,3,1,0:T(8,128)S(1)} %copy-done.8, f32[6,6,8,3,32,1]{4,2,5,3,1,0:T(8,128)S(1)} %copy-done.5, f32[4,4,8,3,32]{4,2,3,1,0:T(8,128)S(1)} %copy-done.17, f32[4,4,8,3,32]{4,2,3,1,0:T(8,128)S(1)} %copy-done.15, ...), kind=kOutput, calls=%fused_computation.29 | convolution fusion | flops 127678464 | bytes 540696 | tf_op jit(solution)/shard_map/transpose(jvp())/conv_general_dilated | solution.py:44
  414.3 4.4 collective-permute-start.46
  420.5 9.3 %fusion.25 = f32[3,3,3,32,32]{4,3,2,1,0:T(8,128)} fusion(f32[6,6,8,3,32,1]{4,2,5,3,1,0:T(8,128)S(1)} %copy-done.3, f32[6,6,8,3,32,1]{4,2,5,3,1,0:T(8,128)S(1)} %copy-done.7, f32[6,6,8,3,32,1]{4,2,5,3,1,0:T(8,128)S(1)} %copy-done.4, f32[4,4,8,3,32]{4,2,3,1,0:T(8,128)S(1)} %convolution_select_fusion.3, f32[4,4,8,3,32]{4,2,3,1,0:T(8,128)S(1)} %copy-done.13, ...), kind=kOutput, calls=%fused_computation.30 | convolution fusion | flops 127678464 | bytes 540696 | tf_op jit(solution)/shard_map/transpose(jvp())/conv_general_dilated | solution.py:44
  430.0 5.3 fusion.30
  435.4 9.2 %fusion.31 = f32[3,3,3,7,32]{4,3,2,1,0:T(8,128)S(1)} fusion(f32[4,4,8,3,32,1]{4,2,5,3,1,0:T(8,128)S(1)} %fusion.30, f32[6,6,8,3,7,1]{2,4,5,3,1,0:T(8,128)S(1)} %fusion.63, f32[6,6,8,3,7,1]{2,4,5,3,1,0:T(8,128)S(1)} %copy-done.6, f32[6,6,8,3,7,1]{2,4,5,3,1,0:T(8,128)S(1)} %copy.404), kind=kOutput, calls=%fused_computation.41 | convolution fusion | flops 27905472 | bytes 145920 | tf_op jit(solution)/shard_map/transpose(jvp())/conv_general_dilated | solution.py:44
  444.6 85.2 %all-reduce = (f32[3,3,3,7,32]{4,3,2,1,0:T(8,128)}, f32[3,3,3,32,1]{3,4,2,1,0:T(1,128)}) all-reduce(f32[3,3,3,7,32]{4,3,2,1,0:T(8,128)S(1)} %fusion.31, f32[3,3,3,32,1]{3,4,2,1,0:T(1,128)S(1)} %fusion.167), channel_id=1, replica_groups=mesh['gx'=16,'gy'=4,'gz'=4] {'gx','gy','gz'}, use_global_device_ids=true, to_apply=%region_9.10 | all-reduce | flops 6912 | bytes 55296 | tf_op jit(solution)/shard_map/psum | solution.py:123
  529.9 160.4 %all-reduce.4.cloned.1.call-done = (f32[3,3,3,32,32]{4,3,2,1,0:T(8,128)}, f32[3,3,3,32,32]{4,3,2,1,0:T(8,128)}) async-done(((f32[3,3,3,32,32]{4,3,2,1,0:T(8,128)}, f32[3,3,3,32,32]{4,3,2,1,0:T(8,128)}), (f32[3,3,3,32,32]{4,3,2,1,0:T(8,128)}, f32[3,3,3,32,32]{4,3,2,1,0:T(8,128)})) %all-reduce.4.cloned.1.call-update) | async-done | bytes 221200 | tf_op jit(solution)/shard_map/psum | solution.py:123
  (269 shorter events, 190.0 us)
Async XLA Ops:
  7.2 683.0 %all-reduce.4.cloned.1.call-start = ((), (), s32[]{:S(2)}) async-start(), calls=%async_computation | async-start | bytes 1769472 | tf_op jit(solution)/shard_map/psum | solution.py:123
  10.6 13.4 %collective-permute-start = (bf16[8,32,4,128]{3,1,2,0:T(8,128)(2,1)S(1)}, bf16[8,32,4,128]{3,1,2,0:T(8,128)(2,1)S(1)}, u32[]{:S(2)}, u32[]{:S(2)}) collective-permute-start(bf16[8,32,4,128]{3,1,2,0:T(8,128)(2,1)S(1)} %copy.435), channel_id=1, source_target_pairs={{0,16},{16,32},{32,48},{48,64},{64,80},{80,96},{96,112},{112,128},... | collective-permute-start | bytes 786440 | tf_op jit(solution)/shard_map/ppermute | solution.py:19
  16.3 13.8 %collective-permute-start.1 = (bf16[8,32,4,128]{3,1,2,0:T(8,128)(2,1)}, bf16[8,32,4,128]{3,1,2,0:T(8,128)(2,1)S(1)}, u32[]{:S(2)}, u32[]{:S(2)}) collective-permute-start(bf16[8,32,4,128]{3,1,2,0:T(8,128)(2,1)} %copy.436), channel_id=1, source_target_pairs={{16,0},{32,16},{48,32},{64,48},{80,64},{96,80},{112,96},{128,112},... | collective-permute-start | bytes 786440 | tf_op jit(solution)/shard_map/ppermute | solution.py:20
  39.4 7.9 %collective-permute-start.2 = (bf16[8,32,40,4]{2,3,1,0:T(4,128)(2,1)S(1)}, bf16[8,32,40,4]{2,3,1,0:T(4,128)(2,1)S(1)}, u32[]{:S(2)}, u32[]{:S(2)}) collective-permute-start(bf16[8,32,40,4]{2,3,1,0:T(4,128)(2,1)S(1)} %get-tuple-element.30), channel_id=1, source_target_pairs={{0,4},{4,8},{8,12},{1,5},{5,9},{9,13},{2,6},{6,10},{10,14},{3,7},{... | collective-permute-start | bytes 245768 | tf_op jit(solution)/shard_map/ppermute | solution.py:19
  42.9 8.5 %collective-permute-start.3 = (bf16[8,32,40,4]{2,3,1,0:T(4,128)(2,1)S(1)}, bf16[8,32,40,4]{2,3,1,0:T(4,128)(2,1)S(1)}, u32[]{:S(2)}, u32[]{:S(2)}) collective-permute-start(bf16[8,32,40,4]{2,3,1,0:T(4,128)(2,1)S(1)} %get-tuple-element.31), channel_id=1, source_target_pairs={{4,0},{8,4},{12,8},{5,1},{9,5},{13,9},{6,2},{10,6},{14,10},{7,3},{... | collective-permute-start | bytes 245768 | tf_op jit(solution)/shard_map/ppermute | solution.py:20
  69.4 24.5 %collective-permute-start.4 = (bf16[8,4,40,136]{3,2,1,0:T(8,128)(2,1)}, bf16[8,4,40,136]{3,2,1,0:T(8,128)(2,1)S(1)}, u32[]{:S(2)}, u32[]{:S(2)}) collective-permute-start(bf16[8,4,40,136]{3,2,1,0:T(8,128)(2,1)} %copy.377), channel_id=1, source_target_pairs={{0,1},{1,2},{2,3},{4,5},{5,6},{6,7},{8,9},{9,10},{10,11},{12,13},{... | collective-permute-start | bytes 1044488 | tf_op jit(solution)/shard_map/ppermute | solution.py:19
  73.9 20.7 %collective-permute-start.5 = (bf16[8,4,40,136]{3,2,1,0:T(8,128)(2,1)}, bf16[8,4,40,136]{3,2,1,0:T(8,128)(2,1)}, u32[]{:S(2)}, u32[]{:S(2)}) collective-permute-start(bf16[8,4,40,136]{3,2,1,0:T(8,128)(2,1)} %copy.379), channel_id=1, source_target_pairs={{1,0},{2,1},{3,2},{5,4},{6,5},{7,6},{9,8},{10,9},{11,10},{13,12},{... | collective-permute-start | bytes 1044488 | tf_op jit(solution)/shard_map/ppermute | solution.py:20
  245.0 6.4 collective-permute-start.12
  254.7 5.5 collective-permute-start.14
  264.4 6.1 collective-permute-start.17
  273.3 6.9 collective-permute-start.18
  290.3 5.5 collective-permute-start.22
  293.2 6.4 collective-permute-start.23
  303.9 5.7 collective-permute-start.24
  320.7 6.1 collective-permute-start.29
  335.2 5.9 collective-permute-start.30
  359.9 7.6 %collective-permute-start.36 = (f32[4,1,16,32]{3,2,1,0:T(8,128)S(1)}, f32[4,1,16,32]{3,2,1,0:T(8,128)S(1)}, u32[]{:S(2)}, u32[]{:S(2)}) collective-permute-start(f32[4,1,16,32]{3,2,1,0:T(8,128)S(1)} %get-tuple-element.76), channel_id=1, source_target_pairs={{0,16},{16,32},{32,48},{48,64},{64,80},{80,96},{96,112},{112,128},... | collective-permute-start | bytes 24584 | tf_op jit(solution)/shard_map/ppermute | solution.py:19
  376.1 11.3 %collective-permute-start.40 = (f32[1,6,18,32]{3,2,1,0:T(8,128)S(1)}, f32[1,6,18,32]{3,2,1,0:T(8,128)S(1)}, u32[]{:S(2)}, u32[]{:S(2)}) collective-permute-start(f32[1,6,18,32]{3,2,1,0:T(8,128)S(1)} %get-tuple-element.56), channel_id=1, source_target_pairs={{0,1},{1,2},{2,3},{4,5},{5,6},{6,7},{8,9},{9,10},{10,11},{12,13},{... | collective-permute-start | bytes 41480 | tf_op jit(solution)/shard_map/ppermute | solution.py:19
  377.8 9.6 %collective-permute-start.41 = (f32[1,6,18,32]{3,2,1,0:T(8,128)S(1)}, f32[1,6,18,32]{3,2,1,0:T(8,128)S(1)}, u32[]{:S(2)}, u32[]{:S(2)}) collective-permute-start(f32[1,6,18,32]{3,2,1,0:T(8,128)S(1)} %get-tuple-element.57), channel_id=1, source_target_pairs={{1,0},{2,1},{3,2},{5,4},{6,5},{7,6},{9,8},{10,9},{11,10},{13,12},{... | collective-permute-start | bytes 41480 | tf_op jit(solution)/shard_map/ppermute | solution.py:20
  392.4 6.9 collective-permute-start.42
  402.0 12.3 %collective-permute-start.44 = (f32[4,6,1,32]{3,2,1,0:T(1,128)S(1)}, f32[4,6,1,32]{3,2,1,0:T(1,128)S(1)}, u32[]{:S(2)}, u32[]{:S(2)}) collective-permute-start(f32[4,6,1,32]{3,2,1,0:T(1,128)S(1)} %get-tuple-element.64), channel_id=1, source_target_pairs={{0,4},{4,8},{8,12},{1,5},{5,9},{9,13},{2,6},{6,10},{10,14},{3,7},{... | collective-permute-start | bytes 9224 | tf_op jit(solution)/shard_map/ppermute | solution.py:19
  403.6 10.7 %collective-permute-start.45 = (f32[4,6,1,32]{3,2,1,0:T(1,128)S(1)}, f32[4,6,1,32]{3,2,1,0:T(1,128)S(1)}, u32[]{:S(2)}, u32[]{:S(2)}) collective-permute-start(f32[4,6,1,32]{3,2,1,0:T(1,128)S(1)} %get-tuple-element.65), channel_id=1, source_target_pairs={{4,0},{8,4},{12,8},{5,1},{9,5},{13,9},{6,2},{10,6},{14,10},{7,3},{... | collective-permute-start | bytes 9224 | tf_op jit(solution)/shard_map/ppermute | solution.py:20
  414.3 15.5 %collective-permute-start.46 = (f32[1,6,18,32]{3,2,1,0:T(8,128)S(1)}, f32[1,6,18,32]{3,2,1,0:T(8,128)S(1)}, u32[]{:S(2)}, u32[]{:S(2)}) collective-permute-start(f32[1,6,18,32]{3,2,1,0:T(8,128)S(1)} %get-tuple-element.54), channel_id=1, source_target_pairs={{0,1},{1,2},{2,3},{4,5},{5,6},{6,7},{8,9},{9,10},{10,11},{12,13},{... | collective-permute-start | bytes 41480 | tf_op jit(solution)/shard_map/ppermute | solution.py:19
  418.7 11.1 %collective-permute-start.47 = (f32[1,6,18,32]{3,2,1,0:T(8,128)S(1)}, f32[1,6,18,32]{3,2,1,0:T(8,128)S(1)}, u32[]{:S(2)}, u32[]{:S(2)}) collective-permute-start(f32[1,6,18,32]{3,2,1,0:T(8,128)S(1)} %get-tuple-element.55), channel_id=1, source_target_pairs={{1,0},{2,1},{3,2},{5,4},{6,5},{7,6},{9,8},{10,9},{11,10},{13,12},{... | collective-permute-start | bytes 41480 | tf_op jit(solution)/shard_map/ppermute | solution.py:20
  (49 other events, 1138.9 us)
Sparse Core Ops, SparseCore 0:
  429.9 260.2 all-reduce.3
where the time goes:
time: 709 us; the launch traced here: 701 us
  waiting for transfers between devices  219 us (31%)
  blocking collectives  167 us (24%)
  starting transfers between devices  107 us (15%)
  other arithmetic  86.5 us (12%)
  matrix products  61.9 us (9%)
  local copies, waits for them, and re-layouts  43.8 us (6%)
  between operations  15.7 us (2%)
    psum x1, waiting for transfers between devices, shards(): lax.psum((gradients[0], gradients[1], gradients[2], gradients[3]), ('gx',...  160 us
    psum x1, blocking collectives, shards(): lax.psum((gradients[0], gradients[1], gradients[2], gradients[3]), ('gx',...  85.2 us
    psum x1, blocking collectives, shards(): totals = lax.psum(squares, ('gx', 'gy', 'gz'))  81.7 us
    ppermute x24, starting transfers between devices, with_halo(): before = lax.ppermute(last, axis, up)  69.8 us
    conv_general_dilated x11, matrix products, valid_conv(): lax.conv_general_dilated(volume[None], kernel, (1, 1, 1), 'VALID', dimens...  61.9 us
    ppermute x24, waiting for transfers between devices, with_halo(): after = lax.ppermute(initial, axis, down)  55.2 us
    ppermute x24, starting transfers between devices, with_halo(): after = lax.ppermute(initial, axis, down)  37.3 us
    concatenate x5, other arithmetic, with_halo(): array = jnp.concatenate([before, array, after], axis=dim)  34.9 us
  transfers between devices with their start and end apart: 49, of which 22 were waited for; matrix products, arithmetic and copies ran while one was open for 12% of the time, Pallas kernels for 0%

commit v1 on v0

v1 whole, which is shorter than its diff:
```python
import itertools

import jax
import jax.numpy as jnp
import numpy as np
from jax import lax
from jax.experimental import pallas as pl
from jax.experimental.pallas import tpu as pltpu
from jax.sharding import PartitionSpec as P

MESH = pl.DeviceIdType.MESH
F32, BF16 = jnp.float32, jnp.bfloat16
SX, SY, SZ = 16, 4, 4
CELLS = 16 * 64 * 64
ROW = 20

tap_offsets = np.arange(16) - 7.5
tap_raw = np.exp(-6.0 * tap_offsets * tap_offsets / 64.0)
filter_taps = tap_raw / tap_raw.sum()


def filter_matrix(fine, coarse):
    out = np.zeros((coarse, fine))
    for j in range(coarse):
        for t in range(16):
            cell = 8 * (j - 1) - 4 + t
            if 0 <= cell < fine:
                out[j, cell] = filter_taps[t]
    return out


def x_filter():
    taps = filter_matrix(32, 6)
    out = np.zeros((6, 8, 8, 32))
    for c in range(8):
        out[:, c, c, :] = taps
    return out.reshape(48, 256).astype(np.float32)


def y_filter():
    taps = filter_matrix(128, 18)
    out = np.zeros((6, 128, 128))
    for x in range(6):
        out[x, :, ROW * x + 1 : ROW * x + 19] = taps.T
    return out.reshape(768, 128).astype(np.float32)


PAIRS = [(a, b) for a, b in itertools.product((-1, 0, 1), repeat=2) if (a, b) != (0, 0)]
GROUPS = {
    (1, 0): (0, 32),
    (-1, 0): (32, 32),
    (0, 1): (64, 8),
    (0, -1): (72, 8),
    (1, 1): (80, 8),
    (1, -1): (88, 8),
    (-1, 1): (96, 8),
    (-1, -1): (104, 8),
}


def packing():
    take = np.zeros((128, 128))
    put = np.zeros((128, 256))
    span = {1: 2, 0: None, -1: 2}
    for (a, b), (start, unused) in GROUPS.items():
        xs = {1: (2, 3), -1: (0, 1), 0: range(4)}[a]
        ys = {1: (14, 15), -1: (0, 1), 0: range(16)}[b]
        for row, (x, y) in enumerate(itertools.product(xs, ys)):
            take[start + row, ROW * (x + 1) + y + 2] = 1
            nx, ny = x - 4 * a, y - 16 * b
            if nx == -2:
                lane = 128 + ny + 2
            elif nx == 5:
                lane = 128 + 100 + ny + 2
            else:
                lane = ROW * (nx + 1) + ny + 2
            put[start + row, lane] = 1
    return take, put


TAKE, PUT = packing()
OFFSETS = [o for o in itertools.product((-1, 0, 1), repeat=3) if o != (0, 0, 0)]
PLANE = [(b, c) for b, c in itertools.product(range(4), repeat=2) if (b, c) != (0, 0)]


def peers():
    out = {(a % SX, b % SY, c % SZ) for a, b, c in OFFSETS}
    out |= {(0, b, c) for b, c in PLANE}
    out |= {(a, 0, 0) for a in range(1, SX)}
    return sorted(out)


PEERS = peers()
TAPS9 = [(dx, dy) for dx in (-1, 0, 1) for dy in (-1, 0, 1)]


def split(value):
    high = value.astype(BF16)
    return high, (value - high.astype(F32)).astype(BF16)


def rolled(value, shift):
    shift = shift % 128
    return value if shift == 0 else pltpu.roll(value, shift, value.ndim - 1)


def mm(a, b):
    return jnp.dot(a, b, preferred_element_type=F32)


def mm_t(a, b):
    return lax.dot_general(a, b, (((1,), (1,)), ((), ())), preferred_element_type=F32)


def kernel(
    fields, mask, ax, gy_mat, w1, w2, w3, lf, lt, b3, b2, take, put,
    pred_out, target_out, g1_out, g2_out, g3_out, g4_out,
    D, L, esend, ypk, RAx, RAz, RY, EW, M1, M2, msend, msend2,
    in_hi, in_lo, h1_hi, h1_lo, sl1, h2, sl2, h2_hi, h2_lo, sl3, h3_hi, h3_lo,
    c3_hi, c3_lo, c3, c2, c2_hi, c2_lo, c1,
    pkB, pkD, RB, RD, FB, FD, cpk, RC, ROT, Chi, Clo,
    GA, GB, RGA, RGB, CA, CB, R2A, R2B, Fs, FULL,
    ssem, rsem,
):
    gx, gy, gz = lax.axis_index("gx"), lax.axis_index("gy"), lax.axis_index("gz")

    def device(a, b, c):
        return (
            lax.rem(gx + (a % SX), SX) if a % SX else gx,
            lax.rem(gy + (b % SY), SY) if b % SY else gy,
            lax.rem(gz + (c % SZ), SZ) if c % SZ else gz,
        )

    def send(src, dst, sem, offset):
        pltpu.make_async_remote_copy(
            src_ref=src, dst_ref=dst, send_sem=ssem.at[sem], recv_sem=rsem.at[sem],
            device_id=device(*offset), device_id_type=MESH,
        ).start()

    def wait_recv(ref, sem):
        pltpu.make_async_copy(ref, ref, rsem.at[sem]).wait()

    def wait_send(ref, sem):
        pltpu.make_async_copy(ref, ref, ssem.at[sem]).wait()

    barrier = pltpu.get_barrier_semaphore()
    for o in PEERS:
        pl.semaphore_signal(barrier, inc=1, device_id=device(*o), device_id_type=MESH)

    lane = lax.broadcasted_iota(jnp.int32, (1, 128), 1)
    sub = lax.broadcasted_iota(jnp.int32, (8, 1), 0)
    xrow = jnp.zeros((1, 128), jnp.int32)
    for j in range(1, 7):
        xrow = xrow + jnp.where(lane >= ROW * j, 1, 0)
    col = lane - ROW * xrow
    inside = jnp.where(lane < 120, 1.0, 0.0)

    def fmask(cond):
        return jnp.where(cond, 1.0, 0.0)

    def flag(cond):
        return jnp.where(cond, 1.0, 0.0).astype(F32)

    okx = {-1: flag(gx > 0), 1: flag(gx < SX - 1)}
    oky = {-1: flag(gy > 0), 1: flag(gy < SY - 1)}
    okz = {-1: flag(gz > 0), 1: flag(gz < SZ - 1), 0: 1.0}
    own = fmask((xrow >= 1) & (xrow <= 4) & (col >= 2) & (col <= 17))
    gyc = gy * 16 + col - 2
    vy = fmask((gyc >= 0) & (gyc < 64))
    gxc = gx * 4 + xrow - 1
    valid0 = fmask((gxc >= 0) & (gxc < 64)) * vy * inside
    valid1 = (fmask(lane < 20) * okx[-1] + fmask((lane >= 100) & (lane < 120)) * okx[1]) * vy

    def zvalid(w):
        g = gz * 4 + w - 2
        return jnp.where((g >= 0) & (g < 16), 1.0, 0.0).astype(F32)

    RB[:, 112:128, :] = jnp.zeros((3, 16, 128), F32)
    RD[:, 112:128, :] = jnp.zeros((3, 16, 128), F32)
    Chi[288:384, :] = jnp.zeros((96, 512), BF16)
    Clo[288:384, :] = jnp.zeros((96, 512), BF16)
    ROT[...] = jnp.zeros((128, 128), F32)
    GA[576:640, :] = jnp.zeros((64, 128), F32)
    GB[72:128, :] = jnp.zeros((56, 128), F32)

    def depth_sums(planes, stores):
        sums = [[None] * 6 for _ in stores]
        for z in range(32):
            values = planes(z)
            for n, value in enumerate(values):
                for j in range(6):
                    t = z - 8 * j + 12
                    if 0 <= t < 16:
                        term = value * float(np.float32(filter_taps[t]))
                        sums[n][j] = term if sums[n][j] is None else sums[n][j] + term
        for n, c in enumerate(stores):
            for j in range(6):
                D[j, c] = sums[n][j]

    def one_field(c, carry):
        depth_sums(lambda z: [fields[c, z].astype(F32)], [c])
        return carry

    lax.fori_loop(0, 6, one_field, 0)

    def sources(z):
        active = mask[z].astype(F32) * fields[0, z].astype(F32)
        source = (active * fields[1, z].astype(F32)).astype(BF16).astype(F32)
        return [active, source]

    depth_sums(sources, [6, 7])

    for j in range(6):
        part = jnp.dot(
            ax[...], D[j].reshape(256, 128), precision=lax.Precision.HIGHEST, preferred_element_type=F32
        )
        for x in range(6):
            L[j * 8 : j * 8 + 8, x * 128 : x * 128 + 128] = part[x * 8 : x * 8 + 8]
    local = jnp.dot(L[...], gy_mat[...], precision=lax.Precision.HIGHEST, preferred_element_type=F32)
    esend[...] = local.reshape(6, 8, 128)

    three = jnp.zeros((1, 128), jnp.int32)
    for j in range(1, 7):
        three = three + jnp.where(col >= 3 * j, 1, 0)
    for n, base in ((0, 16), (1, 1)):
        tile = jnp.zeros((8, 128), F32)
        for j in range(6):
            tile = tile + jnp.where((three == j) & (lane < 120), rolled(esend[j], 3 * j - base), 0.0)
        ypk[n] = tile
    pl.semaphore_wait(barrier, len(PEERS))
    zfrom = {-1: (0, 3), 0: (3, 6), 1: (9, 3)}
    for a, b, c in OFFSETS:
        if b != 0:
            n = 0 if b == 1 else 1
            send(ypk.at[n], RY.at[n, 1 - a, 1 - c], 2, (a, b, c))
        else:
            first, count = {1: (3, 3), -1: (0, 3), 0: (0, 6)}[c]
            if a == 0:
                send(esend.at[pl.ds(first, 3)], RAz.at[0 if c == 1 else 1], 1, (a, b, c))
            else:
                at = zfrom[-c][0]
                send(esend.at[pl.ds(first, count)], RAx.at[0 if a == 1 else 1, pl.ds(at, count)], 0, (a, b, c))
    wait_recv(RAx, 0)
    wait_recv(RAz, 1)
    wait_recv(RY, 2)
    ylow = fmask(col < 3) * inside * oky[-1]
    yhigh = fmask((col >= 17) & (lane < 120)) * oky[1]
    xlow0 = fmask(lane < 40) * okx[-1]
    xlow1 = fmask(lane < 20) * okx[-1]
    xhigh0 = fmask((lane >= 80) & (lane < 120)) * okx[1]
    xhigh1 = fmask((lane >= 100) & (lane < 120)) * okx[1]
    tiles0 = [jnp.zeros((8, 128), F32)] * 8
    tiles1 = [jnp.zeros((8, 128), F32)] * 8
    for c in (-1, 0, 1):
        at, count = zfrom[c]
        zc0 = {-1: 3, 0: 0, 1: 0}[c]
        for i in range(count):
            zc = zc0 + i
            w = {-1: i, 0: zc + 1, 1: 5 + i}[c]
            for a in (-1, 0, 1):
                if a == 0:
                    base = esend[zc] if c == 0 else RAz[0 if c == -1 else 1, i]
                else:
                    base = RAx[0 if a == -1 else 1, at + i]
                full = (
                    base
                    + rolled(RY[0, a + 1, c + 1], -3 * zc) * ylow
                    + rolled(RY[1, a + 1, c + 1], 17 - 3 * zc) * yhigh
                )
                if c != 0:
                    full = full * okz[c]
                if a == 0:
                    tiles0[w] = tiles0[w] + full
                elif a == -1:
                    tiles0[w] = tiles0[w] + rolled(full, -80) * xlow0
                    tiles1[w] = tiles1[w] + rolled(full, -60) * xlow1
                else:
                    tiles0[w] = tiles0[w] + rolled(full, 80) * xhigh0
                    tiles1[w] = tiles1[w] + rolled(full, 60) * xhigh1
    squares = jnp.zeros((8, 128), F32)
    target = jnp.zeros((8, 128), F32)
    for w in range(8):
        EW[w, :, 0:128] = tiles0[w] * (valid0 * zvalid(w))
        EW[w, :, 128:256] = tiles1[w] * (valid1 * zvalid(w))
        if 2 <= w < 6:
            e = tiles0[w] * own
            subgrid = e[7:8] - e[6:7] * e[1:2]
            target = jnp.where(sub == w - 2, subgrid, target)
            values = jnp.where(sub == 7, subgrid, e)
            squares = squares + values * values

    me = gy * 4 + gz
    M1[me] = squares
    msend[...] = squares
    for b, c in PLANE:
        send(msend, M1.at[me], 3, (0, b, c))
    wait_recv(M1.at[0:15], 3)
    squares = jnp.sum(M1[...], axis=0)
    M2[gx] = squares
    msend2[...] = squares
    for a in range(1, SX):
        send(msend2, M2.at[gx], 4, (a, 0, 0))
    wait_recv(M2.at[0:15], 4)
    totals = jnp.sum(jnp.sum(M2[...], axis=0), axis=1, keepdims=True)
    scales = lax.rsqrt(totals / CELLS + 1e-06)
    target = target * scales[7:8]
    scales = jnp.where(sub == 7, 0.0, scales)
    for w in range(8):
        value = jnp.concatenate([EW[w] * scales, jnp.zeros((8, 256), F32)], axis=0)
        in_hi[w], in_lo[w] = split(value)

    def lines(product, k):
        channels = product.shape[0] // 9
        return product[k * channels : (k + 1) * channels]

    def shifted(product):
        sums = []
        for dx in range(3):
            p = [lines(product, dx * 3 + dy) for dy in range(3)]
            sums.append(p[1] + rolled(p[0], 1) + rolled(p[2], -1))
        return sums

    def conv_wide(hi, lo, weights, z):
        high, low = hi[pl.ds(z, 3)], lo[pl.ds(z, 3)]
        high = high.reshape(-1, 256)
        low = low.reshape(-1, 256)
        product = mm(weights[...], jnp.concatenate([high, low, high], axis=0))
        near = shifted(product[:, 0:128])
        far = product[:, 128:256]
        q = [jnp.where(lane < 64, lines(far, dy), lines(far, 6 + dy)) for dy in range(3)]
        edge = q[1] + rolled(q[0], 1) + rolled(q[2], -1)
        return (
            near[1]
            + jnp.where(lane < 20, edge, rolled(near[0], ROW))
            + jnp.where(lane >= 100, edge, rolled(near[2], -ROW))
        )

    def conv_narrow(hi, lo, weights, z):
        def piece(ref):
            left = ref[pl.ds(z, 3), :, 0:128].reshape(-1, 128)
            right = ref[pl.ds(z + 1, 3), :, 0:128].reshape(-1, 128)
            return jnp.concatenate([left, right], axis=1)

        high, low = piece(hi), piece(lo)
        product = mm(weights[...], jnp.concatenate([high, low, high], axis=0))
        outs = []
        for n in range(2):
            near = shifted(product[:, 128 * n : 128 * n + 128])
            outs.append(near[1] + rolled(near[0], ROW) + rolled(near[2], -ROW))
        return outs

    def activate(v):
        sigma = 1.0 / (1.0 + jnp.exp(-v))
        return v * sigma, sigma * (1.0 + v * (1.0 - sigma))

    def first_layer(z, carry):
        h, slope = activate(conv_wide(in_hi, in_lo, w1, z))
        h1_hi[z], h1_lo[z] = split(h * (valid0 * zvalid(z + 1)))
        sl1[z] = slope
        return carry

    lax.fori_loop(0, 6, first_layer, 0)

    def second_layer(q, carry):
        for n, v in enumerate(conv_narrow(h1_hi, h1_lo, w2, 2 * q)):
            h, slope = activate(v)
            h2[2 * q + n] = h * own
            sl2[2 * q + n] = slope * own
        return carry

    lax.fori_loop(0, 2, second_layer, 0)

    group_ok = jnp.zeros((1, 128), F32)
    for (a, b), (start, count) in GROUPS.items():
        okay = 1.0
        if a:
            okay = okay * okx[-a]
        if b:
            okay = okay * oky[-b]
        group_ok = group_ok + fmask((lane >= start) & (lane < start + count)) * okay

    def start_halo(value, packed, received, faces, sem):
        hi, lo = split(value[...].reshape(128, 128))
        t = take[...]
        packed[...] = mm_t(jnp.concatenate([t, t], axis=1), jnp.concatenate([hi, lo], axis=1))
        for a, b, c in OFFSETS:
            if (a, b) == (0, 0):
                src = value.at[pl.ds(2 if c == 1 else 0, 2)]
                send(src, faces.at[0 if c == 1 else 1], sem + 1, (a, b, c))
            else:
                start, count = GROUPS[(a, b)]
                send(
                    packed.at[pl.ds(start, count)],
                    received.at[1 - c, pl.ds(start, count)],
                    sem,
                    (a, b, c),
                )

    def finish_halo(value, received, faces, sem, hi, lo):
        wait_recv(received.at[:, 0:112], sem)
        wait_recv(faces, sem + 1)
        below = received[0].T[64:128] * okz[-1]
        level = received[1].T
        above = received[2].T[0:64] * okz[1]
        rows = jnp.concatenate([below, level, above], axis=0) * group_ok
        rhi, rlo = split(rows)
        p = put[...]
        spread = mm(jnp.concatenate([rhi, rlo], axis=1), jnp.concatenate([p, p], axis=0))
        for w in range(8):
            part = spread[32 * w : 32 * w + 32]
            if w < 2:
                middle = faces[0, w] * okz[-1]
            elif w < 6:
                middle = value[w - 2]
            else:
                middle = faces[1, w - 6] * okz[1]
            hi[w, :, 0:128], lo[w, :, 0:128] = split(part[:, 0:128] + middle)
            hi[w, :, 128:256], lo[w, :, 128:256] = split(part[:, 128:256])

    start_halo(h2, pkB, RB, FB, 5)
    finish_halo(h2, RB, FB, 5, h2_hi, h2_lo)

    def third_layer(z, carry):
        v = conv_wide(h2_hi, h2_lo, w3, z)
        h, slope = activate(v)
        keep = valid0 * zvalid(z + 1)
        h3_hi[z], h3_lo[z] = split(h * keep)
        sl3[z] = slope * keep
        return carry

    lax.fori_loop(0, 6, third_layer, 0)
    high, low = h3_hi[...].reshape(192, 128), h3_lo[...].reshape(192, 128)
    product = mm(lf[...], jnp.concatenate([high, low, high], axis=0))
    near = shifted(product)
    predicted = near[1] + rolled(near[0], ROW) + rolled(near[2], -ROW)
    cot = (2.0 / CELLS) * (predicted - target) * jnp.where(sub < 4, own, 0.0)
    cpk[...] = cot
    slot = {o: n for n, o in enumerate(OFFSETS)}
    for o in OFFSETS:
        send(cpk, RC.at[slot[(-o[0], -o[1], -o[2])]], 7, o)
    for x in range(4):
        at = -(ROW * (x + 1) + 2)
        pred_out[:, x, :] = rolled(predicted, at)[0:4, 0:16]
        target_out[:, x, :] = rolled(target, at)[0:4, 0:16]
    wait_recv(RC, 7)
    cy0 = fmask((col < 2) & (lane < 120)) * oky[-1]
    cy1 = fmask((col >= 18) & (lane < 120)) * oky[1]
    wide0 = jnp.zeros((8, 128), F32)
    wide1 = jnp.zeros((8, 128), F32)
    for c in (-1, 0, 1):
        tile0 = tile1 = None
        for a in (0, -1, 1):
            base = cot if (a, c) == (0, 0) else RC[slot[(a, 0, c)]]
            full = base + rolled(RC[slot[(a, -1, c)]], -16) * cy0 + rolled(RC[slot[(a, 1, c)]], 16) * cy1
            if a == 0:
                tile0, tile1 = full, jnp.zeros((8, 128), F32)
            elif a == -1:
                tile0 = tile0 + rolled(full, -80) * (fmask(lane < 20) * okx[-1])
                tile1 = tile1 + rolled(full, -60) * (fmask(lane < 20) * okx[-1])
            else:
                tile0 = tile0 + rolled(full, 80) * xhigh1
                tile1 = tile1 + rolled(full, 60) * xhigh1
        shift, rows = {-1: (6, sub < 2), 0: (2, (sub >= 2) & (sub < 6)), 1: (6, sub >= 6)}[c]
        wide0 = wide0 + jnp.where(rows, pltpu.roll(tile0, shift, 0), 0.0) * okz[c]
        wide1 = wide1 + jnp.where(rows, pltpu.roll(tile1, shift, 0), 0.0) * okz[c]

    pieces = []
    for dx, dy in TAPS9:
        if dx == 0:
            pieces.append(rolled(wide0, dy))
        elif dx == 1:
            pieces.append(jnp.where(lane < 20, rolled(wide1, dy), rolled(wide0, ROW + dy)))
        else:
            pieces.append(jnp.where(lane >= 100, rolled(wide1, dy), rolled(wide0, dy - ROW)))
    hi, lo = split(jnp.concatenate(pieces, axis=0))
    back = mm(lt[...], jnp.concatenate([hi.astype(F32), lo.astype(F32), hi.astype(F32)], axis=0).astype(BF16))
    for s in range(6):
        value = back[32 * s : 32 * s + 32] * sl3[s]
        c3_hi[s], c3_lo[s] = split(value)
        if 1 <= s < 5:
            c3[s - 1] = value * own

    def second_back(q, carry):
        for n, v in enumerate(conv_narrow(c3_hi, c3_lo, b3, 2 * q)):
            c2[2 * q + n] = v * sl2[2 * q + n]
        return carry

    lax.fori_loop(0, 2, second_back, 0)
    start_halo(c2, pkD, RD, FD, 8)

    def shift_cotangent(value):
        for z in range(4):
            v = value[z]
            for k, (dx, dy) in enumerate(TAPS9):
                at = slice(32 * k, 32 * k + 32)
                Chi[at, 128 * z : 128 * z + 128], Clo[at, 128 * z : 128 * z + 128] = split(
                    rolled(v, ROW * dx + dy)
                )

    def stack(ref, first):
        bands = []
        for dz in range(3):
            bands.append(jnp.concatenate([ref[first + dz + z, :, 0:128] for z in range(4)], axis=1))
        return jnp.concatenate(bands, axis=0)

    def gradient(hi, lo, first, chi, clo):
        high, low = stack(hi, first), stack(lo, first)
        n = high.shape[0]
        both = mm_t(jnp.concatenate([high, low], axis=0), chi)
        return both[0:n] + both[n : 2 * n] + mm_t(high, clo)

    for k, (dx, dy) in enumerate(TAPS9):
        ROT[8 * k : 8 * k + 8, :] = rolled(cot, ROW * dx + dy)
    qhi, qlo = [], []
    for z in range(4):
        hi, lo = split(ROT[pl.ds(z, 16, stride=8), :])
        qhi.append(hi)
        qlo.append(lo)

    def at_lane_64(parts):
        body = jnp.concatenate(parts, axis=1)
        return jnp.concatenate([jnp.zeros((64, 512), BF16), body, jnp.zeros((48, 512), BF16)], axis=0)

    last = gradient(h3_hi, h3_lo, 0, at_lane_64(qhi), at_lane_64(qlo))
    shift_cotangent(c3)
    third = gradient(h2_hi, h2_lo, 1, Chi[...], Clo[...])
    GA[0:96, :] = third[:, 0:128]
    GA[96:192, :] = third[:, 128:256]
    GA[192:288, :] = third[:, 256:384] + last
    shift_cotangent(c2)
    second = gradient(h1_hi, h1_lo, 0, Chi[...], Clo[...])
    for t in range(3):
        GA[288 + 96 * t : 384 + 96 * t, :] = second[:, 128 * t : 128 * t + 128]

    def plane_peer(b, c):
        return lax.rem(gy + b, SY) * 4 + lax.rem(gz + c, SZ)

    for b, c in PLANE:
        start = pl.multiple_of(plane_peer(b, c) * 40, 8)
        send(GA.at[pl.ds(start, 40)], RGA.at[me], 10, (0, b, c))
    RGA[me] = GA[pl.ds(pl.multiple_of(me * 40, 8), 40), :]

    finish_halo(c2, RD, FD, 8, c2_hi, c2_lo)

    def first_back(q, carry):
        for n, v in enumerate(conv_narrow(c2_hi.at[pl.ds(1, 6)], c2_lo.at[pl.ds(1, 6)], b2, 2 * q)):
            c1[2 * q + n] = v * sl1[2 * q + n + 1] * own
        return carry

    lax.fori_loop(0, 2, first_back, 0)
    shift_cotangent(c1)
    first = gradient(in_hi, in_lo, 1, Chi[...], Clo[...])
    for t in range(3):
        for dz in range(3):
            GB[24 * t + 8 * dz : 24 * t + 8 * dz + 8, :] = first[16 * dz : 16 * dz + 8, 128 * t : 128 * t + 128]
    for b, c in PLANE:
        start = pl.multiple_of(plane_peer(b, c) * 8, 8)
        send(GB.at[pl.ds(start, 8)], RGB.at[me], 11, (0, b, c))
    RGB[me] = GB[pl.ds(pl.multiple_of(me * 8, 8), 8), :]

    wait_recv(RGA.at[0:15], 10)
    CA[...] = jnp.sum(RGA[...], axis=0)
    for a in range(1, SX):
        send(CA, R2A.at[gx], 12, (a, 0, 0))
    R2A[gx] = CA[...]
    wait_recv(RGB.at[0:15], 11)
    CB[...] = jnp.sum(RGB[...], axis=0)
    for a in range(1, SX):
        send(CB, R2B.at[gx], 13, (a, 0, 0))
    R2B[gx] = CB[...]
    wait_recv(R2A.at[0:15], 12)
    wait_recv(R2B.at[0:15], 13)
    Fs[0:40, :] = jnp.sum(R2A[...], axis=0)
    Fs[40:48, :] = jnp.sum(R2B[...], axis=0)
    for b, c in PLANE:
        send(Fs, FULL.at[me], 14, (0, b, c))
    FULL[me] = Fs[...]
    wait_recv(FULL.at[0:15], 14)

    def rows_a(start, count):
        return jnp.concatenate(
            [FULL[r // 40, r % 40 : r % 40 + 8, :] for r in range(start, start + count, 8)], axis=0
        )

    for dz in range(3):
        for k in range(9):
            t, at = (32 * k) // 128, (32 * k) % 128
            for base, out in ((0, g3_out), (288, g2_out)):
                block = rows_a(base + 96 * t + 32 * dz, 32)
                out[dz * 9 + k] = rolled(block, -at)[:, 0:32]
            r = 24 * t + 8 * dz
            block = FULL[r // 8, 40:48, :]
            g1_out[dz * 9 + k] = rolled(block, -at)[0:7, 0:32]
    lasts = jnp.concatenate([rows_a(192, 96), jnp.zeros((32, 128), F32)], axis=0).T[64:80]
    for dz in range(3):
        g4_out[dz] = rolled(lasts, -32 * dz)[0:9, 0:32]

    wait_send(RAx, 0)
    wait_send(RAz, 1)
    wait_send(RY, 2)
    wait_send(M1.at[0:15], 3)
    wait_send(M2.at[0:15], 4)
    wait_send(RB.at[:, 0:112], 5)
    wait_send(FB, 6)
    wait_send(RC, 7)
    wait_send(RD.at[:, 0:112], 8)
    wait_send(FD, 9)
    wait_send(RGA.at[0:15], 10)
    wait_send(RGB.at[0:15], 11)
    wait_send(R2A.at[0:15], 12)
    wait_send(R2B.at[0:15], 13)
    wait_send(FULL.at[0:15], 14)


def split_weights(matrix):
    high = lax.reduce_precision(matrix, 8, 7)
    low = matrix - high
    return jnp.concatenate([high, high, low], axis=-1).astype(BF16)


def forward_weights(kernel_array, channels):
    w = kernel_array
    inputs, outputs = w.shape[3], w.shape[4]
    w = jnp.pad(w, ((0, 0), (0, 0), (0, 0), (0, channels - inputs), (0, 0)))
    return split_weights(w.transpose(1, 2, 4, 0, 3).reshape(9 * outputs, 3 * channels))


def backward_weights(kernel_array):
    w = kernel_array[::-1, ::-1, ::-1]
    return split_weights(w.transpose(1, 2, 3, 0, 4).reshape(9 * w.shape[3], 3 * w.shape[4]))


def last_weights(w_last):
    w = w_last.reshape(3, 9, 32)
    ahead = np.zeros((3, 8, 6), np.float32)
    behind = np.zeros((3, 6, 8), np.float32)
    for d in range(3):
        for z in range(4):
            ahead[d, z, z + d] = 1
        for s in range(6):
            if 0 <= s + 2 - d < 8:
                behind[d, s, s + 2 - d] = 1
    lf = jnp.sum(w[:, :, None, None, :] * ahead[:, None, :, :, None], axis=0)
    lt = jnp.sum(w.transpose(0, 2, 1)[:, None, :, :, None] * behind[:, :, None, None, :], axis=0)
    return split_weights(lf.reshape(72, 192)), split_weights(lt.reshape(192, 72))


def shards(fields, phase_mask, w_first, w_second, w_third, w_last):
    lf, lt = last_weights(w_last)
    operands = (
        fields,
        phase_mask,
        jnp.asarray(x_filter()),
        jnp.asarray(y_filter()),
        forward_weights(w_first, 16),
        forward_weights(w_second, 32),
        forward_weights(w_third, 32),
        lf,
        lt,
        backward_weights(w_third),
        backward_weights(w_second),
        jnp.asarray(TAKE, BF16),
        jnp.asarray(PUT, BF16),
    )
    vmem = pltpu.VMEM

    def f(*shape):
        return vmem(shape, F32)

    def b(*shape):
        return vmem(shape, BF16)

    scratch = [
        f(6, 8, 32, 128), f(48, 768), f(6, 8, 128), f(2, 8, 128),
        f(2, 12, 8, 128), f(2, 3, 8, 128), f(2, 3, 3, 8, 128), f(8, 8, 256),
        f(16, 8, 128), f(16, 8, 128), f(8, 128), f(8, 128),
        b(8, 16, 256), b(8, 16, 256), b(6, 32, 128), b(6, 32, 128), f(6, 32, 128),
        f(4, 32, 128), f(4, 32, 128), b(8, 32, 256), b(8, 32, 256),
        f(6, 32, 128), b(6, 32, 128), b(6, 32, 128),
        b(6, 32, 128), b(6, 32, 128), f(4, 32, 128),
        f(4, 32, 128), b(8, 32, 256), b(8, 32, 256), f(4, 32, 128),
        f(128, 128), f(128, 128), f(3, 128, 128), f(3, 128, 128),
        f(2, 2, 32, 128), f(2, 2, 32, 128), f(8, 128), f(26, 8, 128),
        f(128, 128), b(384, 512), b(384, 512),
        f(640, 128), f(128, 128), f(16, 40, 128), f(16, 8, 128),
        f(40, 128), f(8, 128), f(16, 40, 128), f(16, 8, 128), f(48, 128), f(16, 48, 128),
        pltpu.SemaphoreType.DMA((15,)), pltpu.SemaphoreType.DMA((15,)),
    ]
    out_shape = [
        jax.ShapeDtypeStruct(s, F32)
        for s in ((4, 4, 16), (4, 4, 16), (27, 7, 32), (27, 32, 32), (27, 32, 32), (3, 9, 32))
    ]
    spec = pl.BlockSpec(memory_space=pltpu.VMEM)
    predicted, target, g1, g2, g3, g4 = pl.pallas_call(
        kernel,
        out_shape=out_shape,
        in_specs=[spec] * len(operands),
        out_specs=[spec] * len(out_shape),
        scratch_shapes=scratch,
        compiler_params=pltpu.CompilerParams(
            collective_id=0, has_side_effects=True, vmem_limit_bytes=48 * 1024 * 1024
        ),
        name="training_step",
    )(*operands)
    return (
        predicted,
        target,
        g1.reshape(3, 3, 3, 7, 32),
        g2.reshape(3, 3, 3, 32, 32),
        g3.reshape(3, 3, 3, 32, 32),
        g4.reshape(3, 3, 3, 32, 1),
    )


def solution(mesh):
    in_specs = (P(None, "gz", "gx", "gy"), P("gz", "gx", "gy"), P(), P(), P(), P())
    out_specs = (P("gz", "gx", "gy"), P("gz", "gx", "gy"), P(), P(), P(), P())
    return jax.shard_map(shards, mesh=mesh, in_specs=in_specs, out_specs=out_specs, check_vma=False)
```

time: 709 us -> 89.2 us (0.13); the launches traced: 701 us -> 88.9 us
  waiting for transfers between devices: 219 us -> 0 us
  blocking collectives: 167 us -> 0 us
  starting transfers between devices: 107 us -> 0 us
  other arithmetic: 86.5 us -> 5.49 us
  Pallas kernels: 0 us -> 70 us
  matrix products: 61.9 us -> 0 us
  local copies, waits for them, and re-layouts: 43.8 us -> 12.4 us
  between operations: 15.7 us -> 0.96 us
    psum x2 -> x0, blocking collectives: 167 us -> none  [the longest x1 85.2 us: shards(): lax.psum((gradients[0], gradients[1], gradients[2], gradients[3]), ('gx',...]
    psum x1 -> x0, waiting for transfers between devices: 160 us -> none  [shards(): lax.psum((gradients[0], gradients[1], gradients[2], gradients[3]), ('gx',...]
    ppermute x48 -> x0, starting transfers between devices: 107 us -> none  [the longest x24 69.8 us: with_halo(): before = lax.ppermute(last, axis, up)]
    pallas_call x0 -> x1, Pallas kernels: none -> 70 us  [shards(): pl.pallas_call(kernel, out_shape=out_shape, in_specs=[spec] * len(operand...]
    conv_general_dilated x11 -> x0, matrix products: 61.9 us -> none  [valid_conv(): lax.conv_general_dilated(volume[None], kernel, (1, 1, 1), 'VALID', dimens...]
    ppermute x48 -> x0, waiting for transfers between devices: 58.6 us -> none  [the longest x24 55.2 us: with_halo(): after = lax.ppermute(initial, axis, down)]
    concatenate x7 -> x5, other arithmetic: 37.3 us -> 1.73 us  [split_weights(): return jnp.concatenate([high, high, low], axis=-1).astype(BF16)]
    reduce_sum x5 -> x2, other arithmetic: 20.8 us -> 0.98 us  [the longest x1 0.86 us: last_weights(): jnp.sum(w.transpose(0, 2, 1)[:, None, :, :, None] * behind[:, :, None, No...]
  transfers between devices with their start and end apart: 49 -> 0, of which waited for: 22 -> 0; matrix products, arithmetic and copies ran while one was open for 12% -> 0% of each run, Pallas kernels for 0% -> 0%
where the time goes in v1:
time: 89.2 us; the launch traced here: 88.9 us
  Pallas kernels  70 us (78%)
  local copies, waits for them, and re-layouts  12.4 us (14%)
  other arithmetic  5.49 us (6%)
  between operations  0.96 us (1%)
    pallas_call x1, Pallas kernels, shards(): pl.pallas_call(kernel, out_shape=out_shape, in_specs=[spec] * len(operand...  70 us
    unnamed x27, local copies, waits for them, and re-layouts  5.01 us
    reshape x4, local copies, waits for them, and re-layouts, forward_weights(): w.transpose(1, 2, 4, 0, 3).reshape(9 * outputs, 3 * channels)  3.15 us
    another operation x7, other arithmetic  2.76 us
    transpose x4, local copies, waits for them, and re-layouts, forward_weights(): w.transpose(1, 2, 4, 0, 3).reshape(9 * outputs, 3 * channels)  2.44 us

profile of v1, /device:TPU:1, one launch (start us, length us, event | category | flops | bytes accessed | tf_op | source)
XLA Modules:
  0.0 88.9 jit_solution(11093159399960620064)
XLA Ops:
  0.6 0.7 copy.61
  1.4 0.9 multiply_reduce_fusion
  3.4 0.2 reshape.48
  3.9 0.2 pad_maximum_fusion.4.w1
  4.1 0.3 copy.70
  4.4 0.2 reshape.54
  4.7 0.2 copy-done.6
  4.9 0.3 copy.69
  5.3 0.2 reshape.53
  5.5 0.2 pad_maximum_fusion.2
  5.8 0.3 copy.60
  6.0 0.9 %reshape.50 = f32[288,96]{1,0:T(8,128)} reshape(f32[3,3,32,3,32]{4,3,2,1,0:T(4,128)S(1)} %copy.60) | data formatting | bytes 221184 | tf_op jit(solution)/shard_map/reshape | solution.py:625
  7.0 1.7 %reduce-precision_convert_fusion.2 = (bf16[288,96]{1,0:T(8,128)(2,1)S(1)}, bf16[288,96]{1,0:T(8,128)(2,1)}) fusion(f32[288,96]{1,0:T(8,128)} %reshape.50), kind=kLoop, calls=%fused_computation.14 | loop fusion | flops 110592 | bytes 221184 | tf_op jit(solution)/shard_map/convert.12
  8.7 2.1 %copy.59 = f32[3,3,32,3,32]{4,3,2,1,0:T(4,128)} copy(f32[3,3,32,3,32]{2,4,1,0,3:T(8,128)} %bitcast.23) | data formatting | bytes 221184 | tf_op jit(solution)/shard_map/transpose | solution.py:625
  10.8 2.0 %reshape.49 = f32[288,96]{1,0:T(8,128)} reshape(f32[3,3,32,3,32]{4,3,2,1,0:T(4,128)} %copy.59) | data formatting | bytes 221184 | tf_op jit(solution)/shard_map/reshape | solution.py:625
  12.7 0.9 %reduce-precision_convert_fusion.3 = (bf16[288,96]{1,0:T(8,128)(2,1)S(1)}, bf16[288,96]{1,0:T(8,128)(2,1)S(1)}) fusion(f32[288,96]{1,0:T(8,128)} %reshape.49), kind=kLoop, calls=%fused_computation.16 | loop fusion | flops 110592 | bytes 221184 | tf_op jit(solution)/shard_map/convert.15
  13.7 1.1 %pad_maximum_fusion = (bf16[288,288]{1,0:T(8,128)(2,1)S(1)}, bf16[288,288]{1,0:T(8,128)(2,1)S(1)}) fusion(bf16[288,96]{1,0:T(8,128)(2,1)S(1)} %get-tuple-element.49, bf16[288,96]{1,0:T(8,128)(2,1)S(1)} %get-tuple-element.48, bf16[288,96]{1,0:T(8,128)(2,1)} %get-tuple-element.47, bf16[288,96]{1,0:T(8,128)(2,1)S(1)} %get-tuple-element.46), kind=kLoop, calls=%fused_computation.4 | loop fusion | flops 995328 | bytes 552960 | tf_op jit(solution)/shard_map/concatenate | solution.py:618
  14.9 70.0 %training_step.1 = (f32[4,4,16]{2,1,0:T(4,128)S(1)}, f32[4,4,16]{2,1,0:T(4,128)S(1)}, f32[27,7,32]{2,1,0:T(8,128)S(1)}, f32[27,32,32]{2,1,0:T(8,128)S(1)}, f32[2...) custom-call(bf16[6,32,32,128]{3,2,1,0:T(8,128)(2,1)S(1)} %copy-done, s32[32,32,128]{2,1,0:T(8,128)S(1)} %copy-done.1, ...), custom_call_target="tpu_custom_call" | custom-call | tf_op jit(solution)/shard_map/training_step/pallas_call | solution.py:694
  84.9 0.6 copy.72
  85.5 0.6 copy.78
  86.1 0.6 copy.79
  86.7 0.6 copy.80
  87.3 0.8 copy.81
  88.1 0.8 copy.82
  (44 shorter events, 1.5 us)
Async XLA Ops:
  0.6 2.2 %copy-start.9 = (f32[3,8,6]{1,2,0:T(8,128)S(1)}, f32[3,8,6]{1,2,0:T(8,128)}, u32[]{:S(2)}) copy-start(f32[3,8,6]{1,2,0:T(8,128)} %constant.24) | copy-start | bytes 1732
  2.3 1.0 %copy-start.8 = (f32[3,3,3,7,32]{4,3,2,1,0:T(8,128)S(1)}, f32[3,3,3,7,32]{4,3,2,1,0:T(8,128)}, u32[]{:S(2)}) copy-start(f32[3,3,3,7,32]{4,3,2,1,0:T(8,128)} %param.14) | copy-start | bytes 72580
  3.0 1.0 %copy-start.7 = (f32[3,3,3,32,32]{4,3,2,1,0:T(8,128)S(1)}, f32[3,3,3,32,32]{4,3,2,1,0:T(8,128)}, u32[]{:S(2)}) copy-start(f32[3,3,3,32,32]{4,3,2,1,0:T(8,128)} %param.15) | copy-start | bytes 331780
  3.9 1.0 %copy-start.6 = (f32[3,3,3,32,32]{4,3,2,1,0:T(8,128)S(1)}, f32[3,3,3,32,32]{4,3,2,1,0:T(8,128)}, u32[]{:S(2)}) copy-start(f32[3,3,3,32,32]{4,3,2,1,0:T(8,128)} %param.16) | copy-start | bytes 331780
  7.0 7.9 %copy-start = (bf16[6,32,32,128]{3,2,1,0:T(8,128)(2,1)S(1)}, bf16[6,32,32,128]{3,2,1,0:T(8,128)(2,1)}, u32[]{:S(2)}) copy-start(bf16[6,32,32,128]{3,2,1,0:T(8,128)(2,1)} %fields.1) | copy-start | bytes 4718596
  7.0 7.9 %copy-start.1 = (s32[32,32,128]{2,1,0:T(8,128)S(1)}, s32[32,32,128]{2,1,0:T(8,128)}, u32[]{:S(2)}) copy-start(s32[32,32,128]{2,1,0:T(8,128)} %mask.1) | copy-start | bytes 1572868
  7.0 7.9 %copy-start.2 = (f32[768,128]{1,0:T(8,128)S(1)}, f32[768,128]{1,0:T(8,128)}, u32[]{:S(2)}) copy-start(f32[768,128]{1,0:T(8,128)} %constant.19.clone.gy_mat) | copy-start | bytes 1179652
  7.0 7.9 %copy-start.3 = (bf16[128,256]{1,0:T(8,128)(2,1)S(1)}, bf16[128,256]{1,0:T(8,128)(2,1)}, u32[]{:S(2)}) copy-start(bf16[128,256]{1,0:T(8,128)(2,1)} %constant.21.clone.put) | copy-start | bytes 196612
  7.0 7.9 %copy-start.4 = (f32[48,256]{1,0:T(8,128)S(1)}, f32[48,256]{1,0:T(8,128)}, u32[]{:S(2)}) copy-start(f32[48,256]{1,0:T(8,128)} %constant.18.clone.ax) | copy-start | bytes 147460
  7.0 7.9 %copy-start.5 = (bf16[128,128]{1,0:T(8,128)(2,1)S(1)}, bf16[128,128]{1,0:T(8,128)(2,1)}, u32[]{:S(2)}) copy-start(bf16[128,128]{1,0:T(8,128)(2,1)} %constant.20.clone.take) | copy-start | bytes 98308

commit v2 on v1

--- a/solution.py
+++ b/solution.py
@@ -79,18 +79,40 @@
 
 
 TAKE, PUT = packing()
+
+
+def far(*offset):
+    return -sum(min(d % n, -d % n) * step for d, n, step in zip(offset, (SX, SY, SZ), (1, 2, 2)))
+
+
 OFFSETS = [o for o in itertools.product((-1, 0, 1), repeat=3) if o != (0, 0, 0)]
+OFFSETS.sort(key=lambda o: far(*o))
 PLANE = [(b, c) for b, c in itertools.product(range(4), repeat=2) if (b, c) != (0, 0)]
+PLANE.sort(key=lambda o: far(0, *o))
+LINE = sorted(range(1, SX), key=lambda a: far(a, 0, 0))
 
 
 def peers():
     out = {(a % SX, b % SY, c % SZ) for a, b, c in OFFSETS}
     out |= {(0, b, c) for b, c in PLANE}
     out |= {(a, 0, 0) for a in range(1, SX)}
-    return sorted(out)
+    return sorted(sorted(out), key=lambda o: far(*o))
 
 
 PEERS = peers()
+
+
+def last_selection():
+    ahead = np.zeros((6, 9, 8, 32))
+    behind = np.zeros((32, 6, 128))
+    for s, k, d in itertools.product(range(6), range(9), range(3)):
+        if 0 <= s - d < 4:
+            ahead[s, k, s - d, d * 9 + k] = 1
+        behind[d * 9 + k, s, k * 8 + s + 2 - d] = 1
+    return ahead.reshape(432, 32), behind.reshape(32, 768)
+
+
+AHEAD, BEHIND = last_selection()
 TAPS9 = [(dx, dy) for dx in (-1, 0, 1) for dy in (-1, 0, 1)]
 
 
@@ -113,14 +135,16 @@
 
 
 def kernel(
-    fields, mask, ax, gy_mat, w1, w2, w3, lf, lt, b3, b2, take, put,
-    pred_out, target_out, g1_out, g2_out, g3_out, g4_out,
+    fields_in, mask_in, ax_in, gy_in, first_in, second_in, third_in, last_in, take_in, put_in, ahead_in, behind_in,
+    fields_out, sums_out,
+    fields, mask, ax, gy_mat, w_first, w_second, w_third, w_last, take, put, ahead, behind,
+    padded, w1, w2, w3, lf, lt, b3, b2,
     D, L, esend, ypk, RAx, RAz, RY, EW, M1, M2, msend, msend2,
     in_hi, in_lo, h1_hi, h1_lo, sl1, h2, sl2, h2_hi, h2_lo, sl3, h3_hi, h3_lo,
     c3_hi, c3_lo, c3, c2, c2_hi, c2_lo, c1,
     pkB, pkD, RB, RD, FB, FD, cpk, RC, ROT, Chi, Clo,
     GA, GB, RGA, RGB, CA, CB, R2A, R2B, Fs, FULL,
-    ssem, rsem,
+    ssem, rsem, lsem,
 ):
     gx, gy, gz = lax.axis_index("gx"), lax.axis_index("gy"), lax.axis_index("gz")
 
@@ -143,6 +167,18 @@
     def wait_send(ref, sem):
         pltpu.make_async_copy(ref, ref, ssem.at[sem]).wait()
 
+    loads = [
+        pltpu.make_async_copy(src, dst, lsem.at[n])
+        for n, (src, dst) in enumerate(
+            (
+                (fields_in, fields), (mask_in, mask), (ax_in, ax), (gy_in, gy_mat),
+                (first_in, w_first), (second_in, w_second), (third_in, w_third), (last_in, w_last),
+                (take_in, take), (put_in, put), (ahead_in, ahead), (behind_in, behind),
+            )
+        )
+    ]
+    for load in loads:
+        load.start()
     barrier = pltpu.get_barrier_semaphore()
     for o in PEERS:
         pl.semaphore_signal(barrier, inc=1, device_id=device(*o), device_id_type=MESH)
@@ -180,8 +216,43 @@
     Chi[288:384, :] = jnp.zeros((96, 512), BF16)
     Clo[288:384, :] = jnp.zeros((96, 512), BF16)
     ROT[...] = jnp.zeros((128, 128), F32)
-    GA[576:640, :] = jnp.zeros((64, 128), F32)
+    GA[480:512, :] = jnp.zeros((32, 128), F32)
+    padded[...] = jnp.zeros((27, 16, 32), F32)
     GB[72:128, :] = jnp.zeros((56, 128), F32)
+
+    def parts(value):
+        high, low = split(value)
+        high, low = high.astype(F32), low.astype(F32)
+        return jnp.concatenate([high, high, low], axis=1).astype(BF16)
+
+    def ahead_weights(w, out):
+        for k in range(9):
+            stacked = jnp.concatenate([w[k], w[9 + k], w[18 + k]], axis=0)
+            out[32 * k : 32 * k + 32, :] = parts(stacked.T)
+
+    def back_weights(w, out):
+        for k in range(9):
+            out[32 * k : 32 * k + 32, :] = parts(
+                jnp.concatenate([w[26 - k], w[17 - k], w[8 - k]], axis=1)
+            )
+
+    def last_layer_weights():
+        w = jnp.concatenate([w_last[...].reshape(27, 32), jnp.zeros((5, 32), F32)], axis=0)
+        pieces = []
+        for part in split(w):
+            spread = mm(ahead[...], part)
+            pieces.append(jnp.concatenate([spread[72 * n : 72 * n + 72] for n in range(6)], axis=1))
+        lf[...] = jnp.concatenate([pieces[0], pieces[0], pieces[1]], axis=1).astype(BF16)
+        pieces = []
+        for part in split(w.T):
+            spread = mm(part, behind[...])
+            pieces.append(
+                jnp.concatenate([spread[:, 128 * n : 128 * n + 128] for n in range(6)], axis=0)
+            )
+        lt[...] = jnp.concatenate([pieces[0], pieces[0], pieces[1]], axis=1).astype(BF16)
+
+    for load in loads[:4]:
+        load.wait()
 
     def depth_sums(planes, stores):
         sums = [[None] * 6 for _ in stores]
@@ -240,6 +311,12 @@
             else:
                 at = zfrom[-c][0]
                 send(esend.at[pl.ds(first, count)], RAx.at[0 if a == 1 else 1, pl.ds(at, count)], 0, (a, b, c))
+    for load in loads[4:]:
+        load.wait()
+    for k in range(27):
+        padded[k, 0:7, :] = w_first[k]
+    ahead_weights(padded, w1)
+    ahead_weights(w_second, w2)
     wait_recv(RAx, 0)
     wait_recv(RAz, 1)
     wait_recv(RY, 2)
@@ -294,12 +371,16 @@
     msend[...] = squares
     for b, c in PLANE:
         send(msend, M1.at[me], 3, (0, b, c))
+    ahead_weights(w_third, w3)
+    last_layer_weights()
     wait_recv(M1.at[0:15], 3)
     squares = jnp.sum(M1[...], axis=0)
     M2[gx] = squares
     msend2[...] = squares
-    for a in range(1, SX):
+    for a in LINE:
         send(msend2, M2.at[gx], 4, (a, 0, 0))
+    back_weights(w_third, b3)
+    back_weights(w_second, b2)
     wait_recv(M2.at[0:15], 4)
     totals = jnp.sum(jnp.sum(M2[...], axis=0), axis=1, keepdims=True)
     scales = lax.rsqrt(totals / CELLS + 1e-06)
@@ -359,7 +440,7 @@
         sl1[z] = slope
         return carry
 
-    lax.fori_loop(0, 6, first_layer, 0)
+    lax.fori_loop(0, 6, first_layer, 0, unroll=True)
 
     def second_layer(q, carry):
         for n, v in enumerate(conv_narrow(h1_hi, h1_lo, w2, 2 * q)):
@@ -368,7 +449,7 @@
             sl2[2 * q + n] = slope * own
         return carry
 
-    lax.fori_loop(0, 2, second_layer, 0)
+    lax.fori_loop(0, 2, second_layer, 0, unroll=True)
 
     group_ok = jnp.zeros((1, 128), F32)
     for (a, b), (start, count) in GROUPS.items():
@@ -428,7 +509,7 @@
         sl3[z] = slope * keep
         return carry
 
-    lax.fori_loop(0, 6, third_layer, 0)
+    lax.fori_loop(0, 6, third_layer, 0, unroll=True)
     high, low = h3_hi[...].reshape(192, 128), h3_lo[...].reshape(192, 128)
     product = mm(lf[...], jnp.concatenate([high, low, high], axis=0))
     near = shifted(product)
@@ -438,10 +519,8 @@
     slot = {o: n for n, o in enumerate(OFFSETS)}
     for o in OFFSETS:
         send(cpk, RC.at[slot[(-o[0], -o[1], -o[2])]], 7, o)
-    for x in range(4):
-        at = -(ROW * (x + 1) + 2)
-        pred_out[:, x, :] = rolled(predicted, at)[0:4, 0:16]
-        target_out[:, x, :] = rolled(target, at)[0:4, 0:16]
+    fields_out[0] = predicted
+    fields_out[1] = target
     wait_recv(RC, 7)
     cy0 = fmask((col < 2) & (lane < 120)) * oky[-1]
     cy1 = fmask((col >= 18) & (lane < 120)) * oky[1]
@@ -472,8 +551,8 @@
             pieces.append(jnp.where(lane < 20, rolled(wide1, dy), rolled(wide0, ROW + dy)))
         else:
             pieces.append(jnp.where(lane >= 100, rolled(wide1, dy), rolled(wide0, dy - ROW)))
-    hi, lo = split(jnp.concatenate(pieces, axis=0))
-    back = mm(lt[...], jnp.concatenate([hi.astype(F32), lo.astype(F32), hi.astype(F32)], axis=0).astype(BF16))
+    hi, lo = split(jnp.concatenate(pieces + [jnp.zeros((56, 128), F32)], axis=0))
+    back = mm(lt[...], jnp.concatenate([hi, lo, hi], axis=0))
     for s in range(6):
         value = back[32 * s : 32 * s + 32] * sl3[s]
         c3_hi[s], c3_lo[s] = split(value)
@@ -485,7 +564,7 @@
             c2[2 * q + n] = v * sl2[2 * q + n]
         return carry
 
-    lax.fori_loop(0, 2, second_back, 0)
+    lax.fori_loop(0, 2, second_back, 0, unroll=True)
     start_halo(c2, pkD, RD, FD, 8)
 
     def shift_cotangent(value):
@@ -526,19 +605,19 @@
     third = gradient(h2_hi, h2_lo, 1, Chi[...], Clo[...])
     GA[0:96, :] = third[:, 0:128]
     GA[96:192, :] = third[:, 128:256]
-    GA[192:288, :] = third[:, 256:384] + last
     shift_cotangent(c2)
     second = gradient(h1_hi, h1_lo, 0, Chi[...], Clo[...])
-    for t in range(3):
-        GA[288 + 96 * t : 384 + 96 * t, :] = second[:, 128 * t : 128 * t + 128]
+    GA[192:288, :] = second[:, 0:128]
+    GA[288:384, :] = second[:, 128:256]
+    GA[384:480, :] = third[:, 256:384] + rolled(second[:, 256:384], 32) + last
 
     def plane_peer(b, c):
         return lax.rem(gy + b, SY) * 4 + lax.rem(gz + c, SZ)
 
     for b, c in PLANE:
-        start = pl.multiple_of(plane_peer(b, c) * 40, 8)
-        send(GA.at[pl.ds(start, 40)], RGA.at[me], 10, (0, b, c))
-    RGA[me] = GA[pl.ds(pl.multiple_of(me * 40, 8), 40), :]
+        start = pl.multiple_of(plane_peer(b, c) * 32, 8)
+        send(GA.at[pl.ds(start, 32)], RGA.at[me], 10, (0, b, c))
+    RGA[me] = GA[pl.ds(pl.multiple_of(me * 32, 8), 32), :]
 
     finish_halo(c2, RD, FD, 8, c2_hi, c2_lo)
 
@@ -547,7 +626,7 @@
             c1[2 * q + n] = v * sl1[2 * q + n + 1] * own
         return carry
 
-    lax.fori_loop(0, 2, first_back, 0)
+    lax.fori_loop(0, 2, first_back, 0, unroll=True)
     shift_cotangent(c1)
     first = gradient(in_hi, in_lo, 1, Chi[...], Clo[...])
     for t in range(3):
@@ -560,41 +639,24 @@
 
     wait_recv(RGA.at[0:15], 10)
     CA[...] = jnp.sum(RGA[...], axis=0)
-    for a in range(1, SX):
+    for a in LINE:
         send(CA, R2A.at[gx], 12, (a, 0, 0))
     R2A[gx] = CA[...]
     wait_recv(RGB.at[0:15], 11)
     CB[...] = jnp.sum(RGB[...], axis=0)
-    for a in range(1, SX):
+    for a in LINE:
         send(CB, R2B.at[gx], 13, (a, 0, 0))
     R2B[gx] = CB[...]
     wait_recv(R2A.at[0:15], 12)
     wait_recv(R2B.at[0:15], 13)
-    Fs[0:40, :] = jnp.sum(R2A[...], axis=0)
-    Fs[40:48, :] = jnp.sum(R2B[...], axis=0)
+    Fs[0:32, :] = jnp.sum(R2A[...], axis=0)
+    Fs[32:40, :] = jnp.sum(R2B[...], axis=0)
     for b, c in PLANE:
         send(Fs, FULL.at[me], 14, (0, b, c))
     FULL[me] = Fs[...]
     wait_recv(FULL.at[0:15], 14)
 
-    def rows_a(start, count):
-        return jnp.concatenate(
-            [FULL[r // 40, r % 40 : r % 40 + 8, :] for r in range(start, start + count, 8)], axis=0
-        )
-
-    for dz in range(3):
-        for k in range(9):
-            t, at = (32 * k) // 128, (32 * k) % 128
-            for base, out in ((0, g3_out), (288, g2_out)):
-                block = rows_a(base + 96 * t + 32 * dz, 32)
-                out[dz * 9 + k] = rolled(block, -at)[:, 0:32]
-            r = 24 * t + 8 * dz
-            block = FULL[r // 8, 40:48, :]
-            g1_out[dz * 9 + k] = rolled(block, -at)[0:7, 0:32]
-    lasts = jnp.concatenate([rows_a(192, 96), jnp.zeros((32, 128), F32)], axis=0).T[64:80]
-    for dz in range(3):
-        g4_out[dz] = rolled(lasts, -32 * dz)[0:9, 0:32]
-
+    sums_out[...] = FULL[...]
     wait_send(RAx, 0)
     wait_send(RAz, 1)
     wait_send(RY, 2)
@@ -612,55 +674,49 @@
     wait_send(FULL.at[0:15], 14)
 
 
-def split_weights(matrix):
-    high = lax.reduce_precision(matrix, 8, 7)
-    low = matrix - high
-    return jnp.concatenate([high, high, low], axis=-1).astype(BF16)
-
-
-def forward_weights(kernel_array, channels):
-    w = kernel_array
-    inputs, outputs = w.shape[3], w.shape[4]
-    w = jnp.pad(w, ((0, 0), (0, 0), (0, 0), (0, channels - inputs), (0, 0)))
-    return split_weights(w.transpose(1, 2, 4, 0, 3).reshape(9 * outputs, 3 * channels))
-
-
-def backward_weights(kernel_array):
-    w = kernel_array[::-1, ::-1, ::-1]
-    return split_weights(w.transpose(1, 2, 3, 0, 4).reshape(9 * w.shape[3], 3 * w.shape[4]))
-
-
-def last_weights(w_last):
-    w = w_last.reshape(3, 9, 32)
-    ahead = np.zeros((3, 8, 6), np.float32)
-    behind = np.zeros((3, 6, 8), np.float32)
-    for d in range(3):
-        for z in range(4):
-            ahead[d, z, z + d] = 1
-        for s in range(6):
-            if 0 <= s + 2 - d < 8:
-                behind[d, s, s + 2 - d] = 1
-    lf = jnp.sum(w[:, :, None, None, :] * ahead[:, None, :, :, None], axis=0)
-    lt = jnp.sum(w.transpose(0, 2, 1)[:, None, :, :, None] * behind[:, :, None, None, :], axis=0)
-    return split_weights(lf.reshape(72, 192)), split_weights(lt.reshape(192, 72))
+def unpack_kernel(values, sums, pred_out, target_out, g1_out, g2_out, g3_out, g4_out):
+    for x in range(4):
+        at = -(ROW * (x + 1) + 2)
+        pred_out[:, x, :] = rolled(values[0], at)[0:4, 0:16]
+        target_out[:, x, :] = rolled(values[1], at)[0:4, 0:16]
+
+    def rows(start, count):
+        return jnp.concatenate(
+            [sums[r // 32, r % 32 : r % 32 + 8, :] for r in range(start, start + count, 8)], axis=0
+        )
+
+    for dz in range(3):
+        for k in range(9):
+            t, at = (32 * k) // 128, (32 * k) % 128
+            for n, out in enumerate((g3_out, g2_out)):
+                if k < 8:
+                    block = rolled(rows(192 * n + 96 * t + 32 * dz, 32), -at)
+                else:
+                    block = rolled(rows(384 + 32 * dz, 32), -32 * n)
+                out[dz * 9 + k] = block[:, 0:32]
+            r = 24 * t + 8 * dz
+            g1_out[dz * 9 + k] = rolled(sums[r // 8, 32:40, :], -at)[0:7, 0:32]
+    lasts = jnp.concatenate([rows(384, 96), jnp.zeros((32, 128), F32)], axis=0).T[64:80]
+    for dz in range(3):
+        block = rolled(lasts, -32 * dz)
+        for k in range(9):
+            g4_out[dz * 9 + k] = block[k : k + 1, 0:32]
 
 
 def shards(fields, phase_mask, w_first, w_second, w_third, w_last):
-    lf, lt = last_weights(w_last)
     operands = (
         fields,
         phase_mask,
         jnp.asarray(x_filter()),
         jnp.asarray(y_filter()),
-        forward_weights(w_first, 16),
-        forward_weights(w_second, 32),
-        forward_weights(w_third, 32),
-        lf,
-        lt,
-        backward_weights(w_third),
-        backward_weights(w_second),
+        w_first.reshape(27, 7, 32),
+        w_second.reshape(27, 32, 32),
+        w_third.reshape(27, 32, 32),
+        jnp.swapaxes(w_last, 3, 4).reshape(27, 1, 32),
         jnp.asarray(TAKE, BF16),
         jnp.asarray(PUT, BF16),
+        jnp.asarray(AHEAD, BF16),
+        jnp.asarray(BEHIND, BF16),
     )
     vmem = pltpu.VMEM
 
@@ -670,7 +726,9 @@
     def b(*shape):
         return vmem(shape, BF16)
 
-    scratch = [
+    scratch = [vmem(o.shape, o.dtype) for o in operands]
+    scratch += [
+        f(27, 16, 32), b(288, 144), b(288, 288), b(288, 288), b(72, 576), b(192, 384), b(288, 288), b(288, 288),
         f(6, 8, 32, 128), f(48, 768), f(6, 8, 128), f(2, 8, 128),
         f(2, 12, 8, 128), f(2, 3, 8, 128), f(2, 3, 3, 8, 128), f(8, 8, 256),
         f(16, 8, 128), f(16, 8, 128), f(8, 128), f(8, 128),
@@ -682,33 +740,38 @@
         f(128, 128), f(128, 128), f(3, 128, 128), f(3, 128, 128),
         f(2, 2, 32, 128), f(2, 2, 32, 128), f(8, 128), f(26, 8, 128),
         f(128, 128), b(384, 512), b(384, 512),
-        f(640, 128), f(128, 128), f(16, 40, 128), f(16, 8, 128),
-        f(40, 128), f(8, 128), f(16, 40, 128), f(16, 8, 128), f(48, 128), f(16, 48, 128),
-        pltpu.SemaphoreType.DMA((15,)), pltpu.SemaphoreType.DMA((15,)),
-    ]
-    out_shape = [
-        jax.ShapeDtypeStruct(s, F32)
-        for s in ((4, 4, 16), (4, 4, 16), (27, 7, 32), (27, 32, 32), (27, 32, 32), (3, 9, 32))
+        f(512, 128), f(128, 128), f(16, 32, 128), f(16, 8, 128),
+        f(32, 128), f(8, 128), f(16, 32, 128), f(16, 8, 128), f(40, 128), f(16, 40, 128),
+        pltpu.SemaphoreType.DMA((15,)), pltpu.SemaphoreType.DMA((15,)), pltpu.SemaphoreType.DMA((len(operands),)),
     ]
     spec = pl.BlockSpec(memory_space=pltpu.VMEM)
-    predicted, target, g1, g2, g3, g4 = pl.pallas_call(
+    values, sums = pl.pallas_call(
         kernel,
-        out_shape=out_shape,
-        in_specs=[spec] * len(operands),
-        out_specs=[spec] * len(out_shape),
+        out_shape=[jax.ShapeDtypeStruct((2, 8, 128), F32), jax.ShapeDtypeStruct((16, 40, 128), F32)],
+        in_specs=[pl.BlockSpec(memory_space=pltpu.HBM)] * len(operands),
+        out_specs=[spec] * 2,
         scratch_shapes=scratch,
         compiler_params=pltpu.CompilerParams(
-            collective_id=0, has_side_effects=True, vmem_limit_bytes=48 * 1024 * 1024
+            collective_id=0, has_side_effects=True, vmem_limit_bytes=63 * 1024 * 1024
         ),
         name="training_step",
     )(*operands)
+    shapes = ((4, 4, 16), (4, 4, 16), (27, 7, 32), (27, 32, 32), (27, 32, 32), (27, 1, 32))
+    predicted, target, g1, g2, g3, g4 = pl.pallas_call(
+        unpack_kernel,
+        out_shape=[jax.ShapeDtypeStruct(shape, F32) for shape in shapes],
+        in_specs=[spec] * 2,
+        out_specs=[spec] * 6,
+        compiler_params=pltpu.CompilerParams(vmem_limit_bytes=63 * 1024 * 1024),
+        name="unpack_results",
+    )(values, sums)
     return (
         predicted,
         target,
         g1.reshape(3, 3, 3, 7, 32),
         g2.reshape(3, 3, 3, 32, 32),
         g3.reshape(3, 3, 3, 32, 32),
-        g4.reshape(3, 3, 3, 32, 1),
+        jnp.swapaxes(g4.reshape(3, 3, 3, 1, 32), 3, 4),
     )
 
 

time: 89.2 us -> 65.1 us (0.73)
  local copies, waits for them, and re-layouts: 12.4 us -> 0 us
  Pallas kernels: 70 us -> 64.3 us
  other arithmetic: 5.49 us -> 0 us
    pallas_call x1 -> x2, Pallas kernels: 70 us -> 64.3 us  [the longest x1 62.1 us: shards(): pl.pallas_call(kernel, out_shape=[jax.ShapeDtypeStruct((2, 8, 128), F32),...]
    unnamed x27 -> x0, local copies, waits for them, and re-layouts: 5.01 us -> none
    reshape x9 -> x0, local copies, waits for them, and re-layouts: 3.96 us -> none  [the longest x4 3.15 us: forward_weights(): w.transpose(1, 2, 4, 0, 3).reshape(9 * outputs, 3 * channels)]
    transpose x9 -> x0, local copies, waits for them, and re-layouts: 3.12 us -> none  [the longest x4 2.44 us: forward_weights(): w.transpose(1, 2, 4, 0, 3).reshape(9 * outputs, 3 * channels)]
    another operation x7 -> x0, other arithmetic: 2.76 us -> none
    concatenate x5 -> x0, other arithmetic: 1.73 us -> none  [split_weights(): return jnp.concatenate([high, high, low], axis=-1).astype(BF16)]
    reduce_sum x2 -> x0, other arithmetic: 0.98 us -> none  [the longest x1 0.86 us: last_weights(): jnp.sum(w.transpose(0, 2, 1)[:, None, :, :, None] * behind[:, :, None, No...]
where the time goes in v2:
time: 65.1 us; the launch traced here: 64.9 us
  Pallas kernels  64.3 us (99%)
    pallas_call x1, Pallas kernels, shards(): pl.pallas_call(kernel, out_shape=[jax.ShapeDtypeStruct((2, 8, 128), F32),...  62.1 us
    pallas_call x1, Pallas kernels, shards(): pl.pallas_call(unpack_kernel, out_shape=[jax.ShapeDtypeStruct(shape, F32)...  2.2 us

profile of v2, /device:TPU:1, one launch (start us, length us, event | category | flops | bytes accessed | tf_op | source)
XLA Modules:
  0.0 64.9 jit_solution(5377537817440745185)
XLA Ops:
  0.6 62.1 %training_step.1 = (f32[2,8,128]{2,1,0:T(8,128)}, f32[16,40,128]{2,1,0:T(8,128)}) custom-call(bf16[6,32,32,128]{3,2,1,0:T(8,128)(2,1)} %fields_in.1, s32[32,32,128]{2,1,0:T(8,128)} %mask_in.1, f32[48,256]{1,0:T(8,128)} %constant.12.clone.ax_in, f32[768,128]{1,0:T(8,128)} %constant.13.clone.gy_in, f32[27,7,32]{2,1,0:T(8,128)} %bitcast.10, ...), custom_call_target="tpu_custom_call" | custom-call | tf_op jit(solution)/shard_map/training_step/pallas_call | solution.py:748
  62.7 2.2 %unpack_results.1 = (f32[4,4,16]{2,1,0:T(4,128)}, f32[4,4,16]{2,1,0:T(4,128)}, f32[27,7,32]{2,1,0:T(8,128)}, f32[27,32,32]{2,1,0:T(8,128)}, f32[27,32,32]{2,1,0:T(8,128)}, /*index=5*/f32[27,1,32]{2,1,0:T(1,128)}) custom-call(f32[2,8,128]{2,1,0:T(8,128)} %get-tuple-element.14.values, f32[16,40,128]{2,1,0:T(8,128)} %get-tuple-element.15.sums), custom_call_target="tpu_custom_call" | custom-call | tf_op jit(solution)/shard_map/unpack_results/pallas_call | solution.py:760

commit v3 on v2

--- a/solution.py
+++ b/solution.py
@@ -89,6 +89,8 @@
 OFFSETS.sort(key=lambda o: far(*o))
 PLANE = [(b, c) for b, c in itertools.product(range(4), repeat=2) if (b, c) != (0, 0)]
 PLANE.sort(key=lambda o: far(0, *o))
+CLOSE = [(t, b, c) for t, b, c in itertools.product((0, 1), range(4), range(4)) if (t, b, c) != (0, 0, 0)]
+CLOSE.sort(key=lambda o: far(0, o[1], o[2]))
 LINE = sorted(range(1, SX), key=lambda a: far(a, 0, 0))
 
 
@@ -141,9 +143,9 @@
     padded, w1, w2, w3, lf, lt, b3, b2,
     D, L, esend, ypk, RAx, RAz, RY, EW, M1, M2, msend, msend2,
     in_hi, in_lo, h1_hi, h1_lo, sl1, h2, sl2, h2_hi, h2_lo, sl3, h3_hi, h3_lo,
-    c3_hi, c3_lo, c3, c2, c2_hi, c2_lo, c1,
-    pkB, pkD, RB, RD, FB, FD, cpk, RC, ROT, Chi, Clo,
-    GA, GB, RGA, RGB, CA, CB, R2A, R2B, Fs, FULL,
+    c3_hi, c3_lo, c3, c2, c2_hi, c2_lo, c1_hi, c1_lo, near_hi, near_lo,
+    pkB, RB, FB, cpk, RC, ROT, Chi, Clo,
+    GA, GB, RGA, CA, R2A, Fs, FULL,
     ssem, rsem, lsem,
 ):
     gx, gy, gz = lax.axis_index("gx"), lax.axis_index("gy"), lax.axis_index("gz")
@@ -155,10 +157,20 @@
             lax.rem(gz + (c % SZ), SZ) if c % SZ else gz,
         )
 
+    core = lax.rem(gx, 2)
+    twin = gx + 1 - 2 * core
+
+    def close(t, b, c):
+        same = device(0, b, c)
+        return (twin if t else gx,) + same[1:]
+
     def send(src, dst, sem, offset):
+        send_to(src, dst, sem, device(*offset))
+
+    def send_to(src, dst, sem, target):
         pltpu.make_async_remote_copy(
             src_ref=src, dst_ref=dst, send_sem=ssem.at[sem], recv_sem=rsem.at[sem],
-            device_id=device(*offset), device_id_type=MESH,
+            device_id=target, device_id_type=MESH,
         ).start()
 
     def wait_recv(ref, sem):
@@ -182,6 +194,9 @@
     barrier = pltpu.get_barrier_semaphore()
     for o in PEERS:
         pl.semaphore_signal(barrier, inc=1, device_id=device(*o), device_id_type=MESH)
+    twins = [(b, c) for t, b, c in CLOSE if t and 2 in (b, c)]
+    for b, c in twins:
+        pl.semaphore_signal(barrier, inc=1, device_id=close(1, b, c), device_id_type=MESH)
 
     lane = lax.broadcasted_iota(jnp.int32, (1, 128), 1)
     sub = lax.broadcasted_iota(jnp.int32, (8, 1), 0)
@@ -212,13 +227,14 @@
         return jnp.where((g >= 0) & (g < 16), 1.0, 0.0).astype(F32)
 
     RB[:, 112:128, :] = jnp.zeros((3, 16, 128), F32)
-    RD[:, 112:128, :] = jnp.zeros((3, 16, 128), F32)
+    for w in (0, 1, 6, 7):
+        c2_hi[w] = jnp.zeros((32, 128), BF16)
+        c2_lo[w] = jnp.zeros((32, 128), BF16)
     Chi[288:384, :] = jnp.zeros((96, 512), BF16)
     Clo[288:384, :] = jnp.zeros((96, 512), BF16)
     ROT[...] = jnp.zeros((128, 128), F32)
-    GA[480:512, :] = jnp.zeros((32, 128), F32)
     padded[...] = jnp.zeros((27, 16, 32), F32)
-    GB[72:128, :] = jnp.zeros((56, 128), F32)
+    GB[...] = jnp.zeros((128, 128), F32)
 
     def parts(value):
         high, low = split(value)
@@ -298,7 +314,7 @@
         for j in range(6):
             tile = tile + jnp.where((three == j) & (lane < 120), rolled(esend[j], 3 * j - base), 0.0)
         ypk[n] = tile
-    pl.semaphore_wait(barrier, len(PEERS))
+    pl.semaphore_wait(barrier, len(PEERS) + len(twins))
     zfrom = {-1: (0, 3), 0: (3, 6), 1: (9, 3)}
     for a, b, c in OFFSETS:
         if b != 0:
@@ -499,6 +515,20 @@
             hi[w, :, 128:256], lo[w, :, 128:256] = split(part[:, 128:256])
 
     start_halo(h2, pkB, RB, FB, 5)
+
+    for w in range(8):
+        value = EW[w] * scales
+        tile0, tile1 = value[:, 0:128], value[:, 128:256]
+        moved = []
+        for dx, dy in TAPS9:
+            near = rolled(tile0, -ROW * dx - dy)
+            if dx == 1:
+                near = jnp.where(lane >= 100, rolled(tile1, -dy), near)
+            elif dx == -1:
+                near = jnp.where(lane < 20, rolled(tile1, -dy), near)
+            moved.append(near)
+        at = slice(128 * w, 128 * w + 128)
+        near_hi[:, at], near_lo[:, at] = split(jnp.concatenate(moved, axis=0))
     finish_halo(h2, RB, FB, 5, h2_hi, h2_lo)
 
     def third_layer(z, carry):
@@ -561,11 +591,12 @@
 
     def second_back(q, carry):
         for n, v in enumerate(conv_narrow(c3_hi, c3_lo, b3, 2 * q)):
-            c2[2 * q + n] = v * sl2[2 * q + n]
+            value = v * sl2[2 * q + n]
+            c2[2 * q + n] = value
+            c2_hi[2 * q + n + 2], c2_lo[2 * q + n + 2] = split(value)
         return carry
 
     lax.fori_loop(0, 2, second_back, 0, unroll=True)
-    start_halo(c2, pkD, RD, FD, 8)
 
     def shift_cotangent(value):
         for z in range(4):
@@ -607,54 +638,68 @@
     GA[96:192, :] = third[:, 128:256]
     shift_cotangent(c2)
     second = gradient(h1_hi, h1_lo, 0, Chi[...], Clo[...])
-    GA[192:288, :] = second[:, 0:128]
-    GA[288:384, :] = second[:, 128:256]
-    GA[384:480, :] = third[:, 256:384] + rolled(second[:, 256:384], 32) + last
+    GA[224:320, :] = second[:, 0:128]
+    GA[320:416, :] = second[:, 128:256]
+
+    def folded(tile, shifts):
+        total = rolled(tile[0:32], shifts[0])
+        for n in (1, 2):
+            total = total + rolled(tile[32 * n : 32 * n + 32], shifts[n])
+        return total
+
+    GA[192:224, :] = folded(third[:, 256:384], (0, 32, 64)) + folded(last[:, 0:128], (32, 41, 50))
 
     def plane_peer(b, c):
         return lax.rem(gy + b, SY) * 4 + lax.rem(gz + c, SZ)
 
-    for b, c in PLANE:
-        start = pl.multiple_of(plane_peer(b, c) * 32, 8)
-        send(GA.at[pl.ds(start, 32)], RGA.at[me], 10, (0, b, c))
-    RGA[me] = GA[pl.ds(pl.multiple_of(me * 32, 8), 32), :]
-
-    finish_halo(c2, RD, FD, 8, c2_hi, c2_lo)
-
     def first_back(q, carry):
-        for n, v in enumerate(conv_narrow(c2_hi.at[pl.ds(1, 6)], c2_lo.at[pl.ds(1, 6)], b2, 2 * q)):
-            c1[2 * q + n] = v * sl1[2 * q + n + 1] * own
+        for n, v in enumerate(conv_narrow(c2_hi, c2_lo, b2, 2 * q)):
+            at = 2 * q + n
+            c1_hi[at], c1_lo[at] = split(v * sl1[at] * (valid0 * zvalid(at + 1)))
         return carry
 
-    lax.fori_loop(0, 2, first_back, 0, unroll=True)
-    shift_cotangent(c1)
-    first = gradient(in_hi, in_lo, 1, Chi[...], Clo[...])
-    for t in range(3):
-        for dz in range(3):
-            GB[24 * t + 8 * dz : 24 * t + 8 * dz + 8, :] = first[16 * dz : 16 * dz + 8, 128 * t : 128 * t + 128]
-    for b, c in PLANE:
-        start = pl.multiple_of(plane_peer(b, c) * 8, 8)
-        send(GB.at[pl.ds(start, 8)], RGB.at[me], 11, (0, b, c))
-    RGB[me] = GB[pl.ds(pl.multiple_of(me * 8, 8), 8), :]
-
-    wait_recv(RGA.at[0:15], 10)
+    lax.fori_loop(0, 3, first_back, 0, unroll=True)
+
+    def bands(ref):
+        blank = jnp.zeros((32, 128), BF16)
+        return jnp.concatenate(
+            [
+                jnp.concatenate([ref[w - d] if 0 <= w - d < 6 else blank for w in range(8)], axis=1)
+                for d in range(3)
+            ],
+            axis=0,
+        )
+
+    both = mm_t(jnp.concatenate([near_hi[...], near_lo[...]], axis=0), bands(c1_hi))
+    GB[0:72, 0:96] = both[0:72] + both[72:144] + mm_t(near_hi[...], bands(c1_lo))
+    GA[448:512, :] = GB[0:64, :]
+    tail = GB[64:72, :]
+    moved = [
+        rolled(jnp.where((lane >= 32 * d) & (lane < 32 * d + 32), tail, 0.0), 96 - 32 * d) for d in range(3)
+    ]
+    GA[416:448, :] = folded(second[:, 256:384], (0, 32, 64)) + jnp.concatenate(
+        moved + [jnp.zeros((8, 128), F32)], axis=0
+    )
+
+    mine = me * 2 + core
+    for t, b, c in CLOSE:
+        theirs = plane_peer(b, c) * 2 + (1 - core if t else core)
+        start = pl.multiple_of(theirs * 16, 16)
+        send_to(GA.at[pl.ds(start, 16)], RGA.at[mine], 10, close(t, b, c))
+    RGA[mine] = GA[pl.ds(pl.multiple_of(mine * 16, 16), 16), :]
+    wait_recv(RGA.at[0:31], 10)
     CA[...] = jnp.sum(RGA[...], axis=0)
+    chip = lax.div(gx, 2)
     for a in LINE:
-        send(CA, R2A.at[gx], 12, (a, 0, 0))
-    R2A[gx] = CA[...]
-    wait_recv(RGB.at[0:15], 11)
-    CB[...] = jnp.sum(RGB[...], axis=0)
-    for a in LINE:
-        send(CB, R2B.at[gx], 13, (a, 0, 0))
-    R2B[gx] = CB[...]
-    wait_recv(R2A.at[0:15], 12)
-    wait_recv(R2B.at[0:15], 13)
-    Fs[0:32, :] = jnp.sum(R2A[...], axis=0)
-    Fs[32:40, :] = jnp.sum(R2B[...], axis=0)
-    for b, c in PLANE:
-        send(Fs, FULL.at[me], 14, (0, b, c))
-    FULL[me] = Fs[...]
-    wait_recv(FULL.at[0:15], 14)
+        if a % 2 == 0:
+            send(CA, R2A.at[chip], 12, (a, 0, 0))
+    R2A[chip] = CA[...]
+    wait_recv(R2A.at[0:7], 12)
+    Fs[...] = jnp.sum(R2A[...], axis=0)
+    for t, b, c in CLOSE:
+        send_to(Fs, FULL.at[mine], 14, close(t, b, c))
+    FULL[mine] = Fs[...]
+    wait_recv(FULL.at[0:31], 14)
 
     sums_out[...] = FULL[...]
     wait_send(RAx, 0)
@@ -665,13 +710,9 @@
     wait_send(RB.at[:, 0:112], 5)
     wait_send(FB, 6)
     wait_send(RC, 7)
-    wait_send(RD.at[:, 0:112], 8)
-    wait_send(FD, 9)
-    wait_send(RGA.at[0:15], 10)
-    wait_send(RGB.at[0:15], 11)
-    wait_send(R2A.at[0:15], 12)
-    wait_send(R2B.at[0:15], 13)
-    wait_send(FULL.at[0:15], 14)
+    wait_send(RGA.at[0:31], 10)
+    wait_send(R2A.at[0:7], 12)
+    wait_send(FULL.at[0:31], 14)
 
 
 def unpack_kernel(values, sums, pred_out, target_out, g1_out, g2_out, g3_out, g4_out):
@@ -682,7 +723,7 @@
 
     def rows(start, count):
         return jnp.concatenate(
-            [sums[r // 32, r % 32 : r % 32 + 8, :] for r in range(start, start + count, 8)], axis=0
+            [sums[r // 16, r % 16 : r % 16 + 8, :] for r in range(start, start + count, 8)], axis=0
         )
 
     for dz in range(3):
@@ -690,17 +731,18 @@
             t, at = (32 * k) // 128, (32 * k) % 128
             for n, out in enumerate((g3_out, g2_out)):
                 if k < 8:
-                    block = rolled(rows(192 * n + 96 * t + 32 * dz, 32), -at)
+                    block = rolled(rows(224 * n + 96 * t + 32 * dz, 32), -at)
                 else:
-                    block = rolled(rows(384 + 32 * dz, 32), -32 * n)
+                    block = rolled(rows(224 * n + 192, 32), -32 * dz)
                 out[dz * 9 + k] = block[:, 0:32]
-            r = 24 * t + 8 * dz
-            g1_out[dz * 9 + k] = rolled(sums[r // 8, 32:40, :], -at)[0:7, 0:32]
-    lasts = jnp.concatenate([rows(384, 96), jnp.zeros((32, 128), F32)], axis=0).T[64:80]
-    for dz in range(3):
-        block = rolled(lasts, -32 * dz)
-        for k in range(9):
-            g4_out[dz * 9 + k] = block[k : k + 1, 0:32]
+            if k < 8:
+                block = rolled(rows(448 + 8 * k, 8), -32 * dz)
+            else:
+                block = rolled(rows(416 + 8 * dz, 8), -96)
+            g1_out[dz * 9 + k] = block[0:7, 0:32]
+    lasts = rows(192, 32).T[96:128]
+    for tap in range(27):
+        g4_out[tap] = lasts[tap : tap + 1]
 
 
 def shards(fields, phase_mask, w_first, w_second, w_third, w_last):
@@ -736,18 +778,16 @@
         f(4, 32, 128), f(4, 32, 128), b(8, 32, 256), b(8, 32, 256),
         f(6, 32, 128), b(6, 32, 128), b(6, 32, 128),
         b(6, 32, 128), b(6, 32, 128), f(4, 32, 128),
-        f(4, 32, 128), b(8, 32, 256), b(8, 32, 256), f(4, 32, 128),
-        f(128, 128), f(128, 128), f(3, 128, 128), f(3, 128, 128),
-        f(2, 2, 32, 128), f(2, 2, 32, 128), f(8, 128), f(26, 8, 128),
+        f(4, 32, 128), b(8, 32, 128), b(8, 32, 128), b(6, 32, 128), b(6, 32, 128), b(72, 1024), b(72, 1024),
+        f(128, 128), f(3, 128, 128), f(2, 2, 32, 128), f(8, 128), f(26, 8, 128),
         f(128, 128), b(384, 512), b(384, 512),
-        f(512, 128), f(128, 128), f(16, 32, 128), f(16, 8, 128),
-        f(32, 128), f(8, 128), f(16, 32, 128), f(16, 8, 128), f(40, 128), f(16, 40, 128),
+        f(512, 128), f(128, 128), f(32, 16, 128), f(16, 128), f(8, 16, 128), f(16, 128), f(32, 16, 128),
         pltpu.SemaphoreType.DMA((15,)), pltpu.SemaphoreType.DMA((15,)), pltpu.SemaphoreType.DMA((len(operands),)),
     ]
     spec = pl.BlockSpec(memory_space=pltpu.VMEM)
     values, sums = pl.pallas_call(
         kernel,
-        out_shape=[jax.ShapeDtypeStruct((2, 8, 128), F32), jax.ShapeDtypeStruct((16, 40, 128), F32)],
+        out_shape=[jax.ShapeDtypeStruct((2, 8, 128), F32), jax.ShapeDtypeStruct((32, 16, 128), F32)],
         in_specs=[pl.BlockSpec(memory_space=pltpu.HBM)] * len(operands),
         out_specs=[spec] * 2,
         scratch_shapes=scratch,

time: 65.1 us -> 59.3 us (0.911)
  Pallas kernels: 64.3 us -> 58.5 us
    pallas_call x1, Pallas kernels: 62.1 us -> 56.3 us  [shards(): pl.pallas_call(kernel, out_shape=[jax.ShapeDtypeStruct((2, 8, 128), F32),...]
where the time goes in v3:
time: 59.3 us; the launch traced here: 59.1 us
  Pallas kernels  58.5 us (99%)
  between operations  0.64 us (1%)
    pallas_call x1, Pallas kernels, shards(): pl.pallas_call(kernel, out_shape=[jax.ShapeDtypeStruct((2, 8, 128), F32),...  56.3 us
    pallas_call x1, Pallas kernels, shards(): pl.pallas_call(unpack_kernel, out_shape=[jax.ShapeDtypeStruct(shape, F32)...  2.16 us

profile of v3, /device:TPU:1, one launch (start us, length us, event | category | flops | bytes accessed | tf_op | source)
XLA Modules:
  0.0 59.1 jit_solution(12650584114358411795)
XLA Ops:
  0.6 56.3 %training_step.1 = (f32[2,8,128]{2,1,0:T(8,128)}, f32[32,16,128]{2,1,0:T(8,128)}) custom-call(bf16[6,32,32,128]{3,2,1,0:T(8,128)(2,1)} %fields_in.1, s32[32,32,128]{2,1,0:T(8,128)} %mask_in.1, f32[48,256]{1,0:T(8,128)} %constant.12.clone.ax_in, f32[768,128]{1,0:T(8,128)} %constant.13.clone.gy_in, f32[27,7,32]{2,1,0:T(8,128)} %bitcast.10, ...), custom_call_target="tpu_custom_call" | custom-call | tf_op jit(solution)/shard_map/training_step/pallas_call | solution.py:788
  57.0 2.2 %unpack_results.1 = (f32[4,4,16]{2,1,0:T(4,128)}, f32[4,4,16]{2,1,0:T(4,128)}, f32[27,7,32]{2,1,0:T(8,128)}, f32[27,32,32]{2,1,0:T(8,128)}, f32[27,32,32]{2,1,0:T(8,128)}, /*index=5*/f32[27,1,32]{2,1,0:T(1,128)}) custom-call(f32[2,8,128]{2,1,0:T(8,128)} %get-tuple-element.14.values, f32[32,16,128]{2,1,0:T(8,128)} %get-tuple-element.15.sums), custom_call_target="tpu_custom_call" | custom-call | tf_op jit(solution)/shard_map/unpack_results/pallas_call | solution.py:800

commit v4 on v3

--- a/solution.py
+++ b/solution.py
@@ -91,13 +91,13 @@
 PLANE.sort(key=lambda o: far(0, *o))
 CLOSE = [(t, b, c) for t, b, c in itertools.product((0, 1), range(4), range(4)) if (t, b, c) != (0, 0, 0)]
 CLOSE.sort(key=lambda o: far(0, o[1], o[2]))
-LINE = sorted(range(1, SX), key=lambda a: far(a, 0, 0))
+LINE = sorted(range(2, SX, 2), key=lambda a: far(a, 0, 0))
 
 
 def peers():
     out = {(a % SX, b % SY, c % SZ) for a, b, c in OFFSETS}
     out |= {(0, b, c) for b, c in PLANE}
-    out |= {(a, 0, 0) for a in range(1, SX)}
+    out |= {(a, 0, 0) for a in range(2, SX, 2)}
     return sorted(sorted(out), key=lambda o: far(*o))
 
 
@@ -383,21 +383,23 @@
             squares = squares + values * values
 
     me = gy * 4 + gz
-    M1[me] = squares
+    mine = me * 2 + core
+    chip = lax.div(gx, 2)
+    M1[mine] = squares
     msend[...] = squares
-    for b, c in PLANE:
-        send(msend, M1.at[me], 3, (0, b, c))
+    for t, b, c in CLOSE:
+        send_to(msend, M1.at[mine], 3, close(t, b, c))
     ahead_weights(w_third, w3)
     last_layer_weights()
-    wait_recv(M1.at[0:15], 3)
+    wait_recv(M1.at[0:31], 3)
     squares = jnp.sum(M1[...], axis=0)
-    M2[gx] = squares
+    M2[chip] = squares
     msend2[...] = squares
     for a in LINE:
-        send(msend2, M2.at[gx], 4, (a, 0, 0))
+        send(msend2, M2.at[chip], 4, (a, 0, 0))
     back_weights(w_third, b3)
     back_weights(w_second, b2)
-    wait_recv(M2.at[0:15], 4)
+    wait_recv(M2.at[0:7], 4)
     totals = jnp.sum(jnp.sum(M2[...], axis=0), axis=1, keepdims=True)
     scales = lax.rsqrt(totals / CELLS + 1e-06)
     target = target * scales[7:8]
@@ -681,7 +683,6 @@
         moved + [jnp.zeros((8, 128), F32)], axis=0
     )
 
-    mine = me * 2 + core
     for t, b, c in CLOSE:
         theirs = plane_peer(b, c) * 2 + (1 - core if t else core)
         start = pl.multiple_of(theirs * 16, 16)
@@ -689,10 +690,8 @@
     RGA[mine] = GA[pl.ds(pl.multiple_of(mine * 16, 16), 16), :]
     wait_recv(RGA.at[0:31], 10)
     CA[...] = jnp.sum(RGA[...], axis=0)
-    chip = lax.div(gx, 2)
     for a in LINE:
-        if a % 2 == 0:
-            send(CA, R2A.at[chip], 12, (a, 0, 0))
+        send(CA, R2A.at[chip], 12, (a, 0, 0))
     R2A[chip] = CA[...]
     wait_recv(R2A.at[0:7], 12)
     Fs[...] = jnp.sum(R2A[...], axis=0)
@@ -705,8 +704,8 @@
     wait_send(RAx, 0)
     wait_send(RAz, 1)
     wait_send(RY, 2)
-    wait_send(M1.at[0:15], 3)
-    wait_send(M2.at[0:15], 4)
+    wait_send(M1.at[0:31], 3)
+    wait_send(M2.at[0:7], 4)
     wait_send(RB.at[:, 0:112], 5)
     wait_send(FB, 6)
     wait_send(RC, 7)
@@ -715,34 +714,48 @@
     wait_send(FULL.at[0:31], 14)
 
 
-def unpack_kernel(values, sums, pred_out, target_out, g1_out, g2_out, g3_out, g4_out):
-    for x in range(4):
-        at = -(ROW * (x + 1) + 2)
-        pred_out[:, x, :] = rolled(values[0], at)[0:4, 0:16]
-        target_out[:, x, :] = rolled(values[1], at)[0:4, 0:16]
+def unpack_kernel(values, sums, pred_to, target_to, g1_to, g2_to, g3_to, g4_to, pred, target, g1, g2, g3, g4, sem):
+    copies = []
+
+    def put(src, dst):
+        copies.append(pltpu.make_async_copy(src, dst, sem.at[len(copies)]))
+        copies[-1].start()
 
     def rows(start, count):
         return jnp.concatenate(
             [sums[r // 16, r % 16 : r % 16 + 8, :] for r in range(start, start + count, 8)], axis=0
         )
 
-    for dz in range(3):
-        for k in range(9):
-            t, at = (32 * k) // 128, (32 * k) % 128
-            for n, out in enumerate((g3_out, g2_out)):
+    for n, (out, to) in enumerate(((g3, g3_to), (g2, g2_to))):
+        for dz in range(3):
+            for k in range(9):
+                t, at = (32 * k) // 128, (32 * k) % 128
                 if k < 8:
                     block = rolled(rows(224 * n + 96 * t + 32 * dz, 32), -at)
                 else:
                     block = rolled(rows(224 * n + 192, 32), -32 * dz)
                 out[dz * 9 + k] = block[:, 0:32]
+            put(out.at[pl.ds(9 * dz, 9)], to.at[pl.ds(9 * dz, 9)])
+    for dz in range(3):
+        for k in range(9):
             if k < 8:
                 block = rolled(rows(448 + 8 * k, 8), -32 * dz)
             else:
                 block = rolled(rows(416 + 8 * dz, 8), -96)
-            g1_out[dz * 9 + k] = block[0:7, 0:32]
+            g1[dz * 9 + k] = block[0:7, 0:32]
+    put(g1, g1_to)
     lasts = rows(192, 32).T[96:128]
     for tap in range(27):
-        g4_out[tap] = lasts[tap : tap + 1]
+        g4[tap] = lasts[tap : tap + 1]
+    put(g4, g4_to)
+    for x in range(4):
+        at = -(ROW * (x + 1) + 2)
+        pred[:, x, :] = rolled(values[0], at)[0:4, 0:16]
+        target[:, x, :] = rolled(values[1], at)[0:4, 0:16]
+    put(pred, pred_to)
+    put(target, target_to)
+    for copy in copies:
+        copy.wait()
 
 
 def shards(fields, phase_mask, w_first, w_second, w_third, w_last):
@@ -773,7 +786,7 @@
         f(27, 16, 32), b(288, 144), b(288, 288), b(288, 288), b(72, 576), b(192, 384), b(288, 288), b(288, 288),
         f(6, 8, 32, 128), f(48, 768), f(6, 8, 128), f(2, 8, 128),
         f(2, 12, 8, 128), f(2, 3, 8, 128), f(2, 3, 3, 8, 128), f(8, 8, 256),
-        f(16, 8, 128), f(16, 8, 128), f(8, 128), f(8, 128),
+        f(32, 8, 128), f(8, 8, 128), f(8, 128), f(8, 128),
         b(8, 16, 256), b(8, 16, 256), b(6, 32, 128), b(6, 32, 128), f(6, 32, 128),
         f(4, 32, 128), f(4, 32, 128), b(8, 32, 256), b(8, 32, 256),
         f(6, 32, 128), b(6, 32, 128), b(6, 32, 128),
@@ -801,7 +814,8 @@
         unpack_kernel,
         out_shape=[jax.ShapeDtypeStruct(shape, F32) for shape in shapes],
         in_specs=[spec] * 2,
-        out_specs=[spec] * 6,
+        out_specs=[pl.BlockSpec(memory_space=pltpu.HBM)] * 6,
+        scratch_shapes=[vmem(shape, F32) for shape in shapes] + [pltpu.SemaphoreType.DMA((10,))],
         compiler_params=pltpu.CompilerParams(vmem_limit_bytes=63 * 1024 * 1024),
         name="unpack_results",
     )(values, sums)

time: 59.3 us -> 59 us (level)
  no operation moved by 1% of the time
where the time goes in v4:
time: 59 us; the launch traced here: 58.9 us
  Pallas kernels  58.2 us (99%)
  between operations  0.64 us (1%)
    pallas_call x1, Pallas kernels, shards(): pl.pallas_call(kernel, out_shape=[jax.ShapeDtypeStruct((2, 8, 128), F32),...  56.2 us
    pallas_call x1, Pallas kernels, shards(): pl.pallas_call(unpack_kernel, out_shape=[jax.ShapeDtypeStruct(shape, F32)...  2.08 us

profile of v4, /device:TPU:1, one launch (start us, length us, event | category | flops | bytes accessed | tf_op | source)
XLA Modules:
  0.0 58.9 jit_solution(15899786397035006725)
XLA Ops:
  0.6 56.2 %training_step.1 = (f32[2,8,128]{2,1,0:T(8,128)}, f32[32,16,128]{2,1,0:T(8,128)}) custom-call(bf16[6,32,32,128]{3,2,1,0:T(8,128)(2,1)} %fields_in.1, s32[32,32,128]{2,1,0:T(8,128)} %mask_in.1, f32[48,256]{1,0:T(8,128)} %constant.12.clone.ax_in, f32[768,128]{1,0:T(8,128)} %constant.13.clone.gy_in, f32[27,7,32]{2,1,0:T(8,128)} %bitcast.10, ...), custom_call_target="tpu_custom_call" | custom-call | tf_op jit(solution)/shard_map/training_step/pallas_call | solution.py:801
  56.8 2.1 %unpack_results.1 = (f32[4,4,16]{2,1,0:T(4,128)}, f32[4,4,16]{2,1,0:T(4,128)}, f32[27,7,32]{2,1,0:T(8,128)}, f32[27,32,32]{2,1,0:T(8,128)}, f32[27,32,32]{2,1,0:T(8,128)}, /*index=5*/f32[27,1,32]{2,1,0:T(1,128)}) custom-call(f32[2,8,128]{2,1,0:T(8,128)} %get-tuple-element.14.values, f32[32,16,128]{2,1,0:T(8,128)} %get-tuple-element.15.sums), custom_call_target="tpu_custom_call" | custom-call | tf_op jit(solution)/shard_map/unpack_results/pallas_call | solution.py:813

commit v5 on v3

--- a/solution.py
+++ b/solution.py
@@ -91,13 +91,13 @@
 PLANE.sort(key=lambda o: far(0, *o))
 CLOSE = [(t, b, c) for t, b, c in itertools.product((0, 1), range(4), range(4)) if (t, b, c) != (0, 0, 0)]
 CLOSE.sort(key=lambda o: far(0, o[1], o[2]))
-LINE = sorted(range(1, SX), key=lambda a: far(a, 0, 0))
+LINE = sorted(range(2, SX, 2), key=lambda a: far(a, 0, 0))
 
 
 def peers():
     out = {(a % SX, b % SY, c % SZ) for a, b, c in OFFSETS}
     out |= {(0, b, c) for b, c in PLANE}
-    out |= {(a, 0, 0) for a in range(1, SX)}
+    out |= {(a, 0, 0) for a in range(2, SX, 2)}
     return sorted(sorted(out), key=lambda o: far(*o))
 
 
@@ -144,8 +144,8 @@
     D, L, esend, ypk, RAx, RAz, RY, EW, M1, M2, msend, msend2,
     in_hi, in_lo, h1_hi, h1_lo, sl1, h2, sl2, h2_hi, h2_lo, sl3, h3_hi, h3_lo,
     c3_hi, c3_lo, c3, c2, c2_hi, c2_lo, c1_hi, c1_lo, near_hi, near_lo,
-    pkB, RB, FB, cpk, RC, ROT, Chi, Clo,
-    GA, GB, RGA, CA, R2A, Fs, FULL,
+    pkB, RB, FB, cpk, RC, ROT, near1_hi, near1_lo, near2_hi, near2_lo,
+    GA, RGA, CA, R2A, Fs, FULL,
     ssem, rsem, lsem,
 ):
     gx, gy, gz = lax.axis_index("gx"), lax.axis_index("gy"), lax.axis_index("gz")
@@ -230,11 +230,8 @@
     for w in (0, 1, 6, 7):
         c2_hi[w] = jnp.zeros((32, 128), BF16)
         c2_lo[w] = jnp.zeros((32, 128), BF16)
-    Chi[288:384, :] = jnp.zeros((96, 512), BF16)
-    Clo[288:384, :] = jnp.zeros((96, 512), BF16)
     ROT[...] = jnp.zeros((128, 128), F32)
     padded[...] = jnp.zeros((27, 16, 32), F32)
-    GB[...] = jnp.zeros((128, 128), F32)
 
     def parts(value):
         high, low = split(value)
@@ -383,21 +380,23 @@
             squares = squares + values * values
 
     me = gy * 4 + gz
-    M1[me] = squares
+    mine = me * 2 + core
+    chip = lax.div(gx, 2)
+    M1[mine] = squares
     msend[...] = squares
-    for b, c in PLANE:
-        send(msend, M1.at[me], 3, (0, b, c))
+    for t, b, c in CLOSE:
+        send_to(msend, M1.at[mine], 3, close(t, b, c))
     ahead_weights(w_third, w3)
     last_layer_weights()
-    wait_recv(M1.at[0:15], 3)
+    wait_recv(M1.at[0:31], 3)
     squares = jnp.sum(M1[...], axis=0)
-    M2[gx] = squares
+    M2[chip] = squares
     msend2[...] = squares
     for a in LINE:
-        send(msend2, M2.at[gx], 4, (a, 0, 0))
+        send(msend2, M2.at[chip], 4, (a, 0, 0))
     back_weights(w_third, b3)
     back_weights(w_second, b2)
-    wait_recv(M2.at[0:15], 4)
+    wait_recv(M2.at[0:7], 4)
     totals = jnp.sum(jnp.sum(M2[...], axis=0), axis=1, keepdims=True)
     scales = lax.rsqrt(totals / CELLS + 1e-06)
     target = target * scales[7:8]
@@ -516,6 +515,16 @@
 
     start_halo(h2, pkB, RB, FB, 5)
 
+    def under_taps(hi, lo, first, out_hi, out_lo):
+        for w in range(6):
+            value = hi[first + w, :, 0:128].astype(F32) + lo[first + w, :, 0:128].astype(F32)
+            at = slice(128 * w, 128 * w + 128)
+            for k, (dx, dy) in enumerate(TAPS9):
+                line = slice(32 * k, 32 * k + 32)
+                out_hi[line, at], out_lo[line, at] = split(rolled(value, -ROW * dx - dy))
+
+    under_taps(h1_hi, h1_lo, 0, near1_hi, near1_lo)
+
     for w in range(8):
         value = EW[w] * scales
         tile0, tile1 = value[:, 0:128], value[:, 128:256]
@@ -551,6 +560,7 @@
         send(cpk, RC.at[slot[(-o[0], -o[1], -o[2])]], 7, o)
     fields_out[0] = predicted
     fields_out[1] = target
+    under_taps(h2_hi, h2_lo, 1, near2_hi, near2_lo)
     wait_recv(RC, 7)
     cy0 = fmask((col < 2) & (lane < 120)) * oky[-1]
     cy1 = fmask((col >= 18) & (lane < 120)) * oky[1]
@@ -598,15 +608,6 @@
 
     lax.fori_loop(0, 2, second_back, 0, unroll=True)
 
-    def shift_cotangent(value):
-        for z in range(4):
-            v = value[z]
-            for k, (dx, dy) in enumerate(TAPS9):
-                at = slice(32 * k, 32 * k + 32)
-                Chi[at, 128 * z : 128 * z + 128], Clo[at, 128 * z : 128 * z + 128] = split(
-                    rolled(v, ROW * dx + dy)
-                )
-
     def stack(ref, first):
         bands = []
         for dz in range(3):
@@ -632,14 +633,28 @@
         return jnp.concatenate([jnp.zeros((64, 512), BF16), body, jnp.zeros((48, 512), BF16)], axis=0)
 
     last = gradient(h3_hi, h3_lo, 0, at_lane_64(qhi), at_lane_64(qlo))
-    shift_cotangent(c3)
-    third = gradient(h2_hi, h2_lo, 1, Chi[...], Clo[...])
-    GA[0:96, :] = third[:, 0:128]
-    GA[96:192, :] = third[:, 128:256]
-    shift_cotangent(c2)
-    second = gradient(h1_hi, h1_lo, 0, Chi[...], Clo[...])
-    GA[224:320, :] = second[:, 0:128]
-    GA[320:416, :] = second[:, 128:256]
+
+    def bands(slabs, count):
+        blank = jnp.zeros((32, 128), BF16)
+        rows = [
+            jnp.concatenate([slabs[w - d] if 0 <= w - d < len(slabs) else blank for w in range(count)], axis=1)
+            for d in range(3)
+        ]
+        return jnp.concatenate(rows + [jnp.zeros((32, 128 * count), BF16)], axis=0)
+
+    def tap_gradient(near_hi, near_lo, parts, count):
+        n = near_hi.shape[0]
+        high = bands([p[0] for p in parts], count)
+        low = bands([p[1] for p in parts], count)
+        both = mm_t(jnp.concatenate([near_hi[...], near_lo[...]], axis=0), high)
+        return both[0:n] + both[n : 2 * n] + mm_t(near_hi[...], low)
+
+    def side(block, d):
+        return rolled(jnp.where((lane >= 32 * d) & (lane < 32 * d + 32), block, 0.0), 96 - 32 * d)
+
+    def store(grad, base, rest):
+        extra = [side(grad[224 + 32 * n : 256 + 32 * n], d) for n in range(2) for d in range(3)]
+        GA[base : base + 224, :] = grad[0:224] + jnp.concatenate(extra + [rest], axis=0)
 
     def folded(tile, shifts):
         total = rolled(tile[0:32], shifts[0])
@@ -647,7 +662,9 @@
             total = total + rolled(tile[32 * n : 32 * n + 32], shifts[n])
         return total
 
-    GA[192:224, :] = folded(third[:, 256:384], (0, 32, 64)) + folded(last[:, 0:128], (32, 41, 50))
+    third = tap_gradient(near2_hi, near2_lo, [split(c3[z]) for z in range(4)], 6)
+    store(third, 0, folded(last[:, 0:128], (32, 41, 50)))
+    second = tap_gradient(near1_hi, near1_lo, [split(c2[z]) for z in range(4)], 6)
 
     def plane_peer(b, c):
         return lax.rem(gy + b, SY) * 4 + lax.rem(gz + c, SZ)
@@ -660,28 +677,10 @@
 
     lax.fori_loop(0, 3, first_back, 0, unroll=True)
 
-    def bands(ref):
-        blank = jnp.zeros((32, 128), BF16)
-        return jnp.concatenate(
-            [
-                jnp.concatenate([ref[w - d] if 0 <= w - d < 6 else blank for w in range(8)], axis=1)
-                for d in range(3)
-            ],
-            axis=0,
-        )
-
-    both = mm_t(jnp.concatenate([near_hi[...], near_lo[...]], axis=0), bands(c1_hi))
-    GB[0:72, 0:96] = both[0:72] + both[72:144] + mm_t(near_hi[...], bands(c1_lo))
-    GA[448:512, :] = GB[0:64, :]
-    tail = GB[64:72, :]
-    moved = [
-        rolled(jnp.where((lane >= 32 * d) & (lane < 32 * d + 32), tail, 0.0), 96 - 32 * d) for d in range(3)
-    ]
-    GA[416:448, :] = folded(second[:, 256:384], (0, 32, 64)) + jnp.concatenate(
-        moved + [jnp.zeros((8, 128), F32)], axis=0
-    )
-
-    mine = me * 2 + core
+    first = tap_gradient(near_hi, near_lo, [(c1_hi[n], c1_lo[n]) for n in range(6)], 8)
+    GA[448:512, :] = first[0:64]
+    store(second, 224, jnp.concatenate([side(first[64:72], d) for d in range(3)] + [jnp.zeros((8, 128), F32)], axis=0))
+
     for t, b, c in CLOSE:
         theirs = plane_peer(b, c) * 2 + (1 - core if t else core)
         start = pl.multiple_of(theirs * 16, 16)
@@ -689,10 +688,8 @@
     RGA[mine] = GA[pl.ds(pl.multiple_of(mine * 16, 16), 16), :]
     wait_recv(RGA.at[0:31], 10)
     CA[...] = jnp.sum(RGA[...], axis=0)
-    chip = lax.div(gx, 2)
     for a in LINE:
-        if a % 2 == 0:
-            send(CA, R2A.at[chip], 12, (a, 0, 0))
+        send(CA, R2A.at[chip], 12, (a, 0, 0))
     R2A[chip] = CA[...]
     wait_recv(R2A.at[0:7], 12)
     Fs[...] = jnp.sum(R2A[...], axis=0)
@@ -705,8 +702,8 @@
     wait_send(RAx, 0)
     wait_send(RAz, 1)
     wait_send(RY, 2)
-    wait_send(M1.at[0:15], 3)
-    wait_send(M2.at[0:15], 4)
+    wait_send(M1.at[0:31], 3)
+    wait_send(M2.at[0:7], 4)
     wait_send(RB.at[:, 0:112], 5)
     wait_send(FB, 6)
     wait_send(RC, 7)
@@ -728,12 +725,11 @@
 
     for dz in range(3):
         for k in range(9):
-            t, at = (32 * k) // 128, (32 * k) % 128
             for n, out in enumerate((g3_out, g2_out)):
-                if k < 8:
-                    block = rolled(rows(224 * n + 96 * t + 32 * dz, 32), -at)
+                if k < 7:
+                    block = rolled(rows(224 * n + 32 * k, 32), -32 * dz)
                 else:
-                    block = rolled(rows(224 * n + 192, 32), -32 * dz)
+                    block = rolled(rows(224 * n + 96 * (k - 7) + 32 * dz, 32), -96)
                 out[dz * 9 + k] = block[:, 0:32]
             if k < 8:
                 block = rolled(rows(448 + 8 * k, 8), -32 * dz)
@@ -773,15 +769,15 @@
         f(27, 16, 32), b(288, 144), b(288, 288), b(288, 288), b(72, 576), b(192, 384), b(288, 288), b(288, 288),
         f(6, 8, 32, 128), f(48, 768), f(6, 8, 128), f(2, 8, 128),
         f(2, 12, 8, 128), f(2, 3, 8, 128), f(2, 3, 3, 8, 128), f(8, 8, 256),
-        f(16, 8, 128), f(16, 8, 128), f(8, 128), f(8, 128),
+        f(32, 8, 128), f(8, 8, 128), f(8, 128), f(8, 128),
         b(8, 16, 256), b(8, 16, 256), b(6, 32, 128), b(6, 32, 128), f(6, 32, 128),
         f(4, 32, 128), f(4, 32, 128), b(8, 32, 256), b(8, 32, 256),
         f(6, 32, 128), b(6, 32, 128), b(6, 32, 128),
         b(6, 32, 128), b(6, 32, 128), f(4, 32, 128),
         f(4, 32, 128), b(8, 32, 128), b(8, 32, 128), b(6, 32, 128), b(6, 32, 128), b(72, 1024), b(72, 1024),
         f(128, 128), f(3, 128, 128), f(2, 2, 32, 128), f(8, 128), f(26, 8, 128),
-        f(128, 128), b(384, 512), b(384, 512),
-        f(512, 128), f(128, 128), f(32, 16, 128), f(16, 128), f(8, 16, 128), f(16, 128), f(32, 16, 128),
+        f(128, 128), b(288, 768), b(288, 768), b(288, 768), b(288, 768),
+        f(512, 128), f(32, 16, 128), f(16, 128), f(8, 16, 128), f(16, 128), f(32, 16, 128),
         pltpu.SemaphoreType.DMA((15,)), pltpu.SemaphoreType.DMA((15,)), pltpu.SemaphoreType.DMA((len(operands),)),
     ]
     spec = pl.BlockSpec(memory_space=pltpu.VMEM)

time: 59.3 us -> 59.2 us (level)
  no operation moved by 1% of the time
where the time goes in v5:
time: 59.2 us; the launch traced here: 59.1 us
  Pallas kernels  58.4 us (99%)
  between operations  0.64 us (1%)
    pallas_call x1, Pallas kernels, shards(): pl.pallas_call(kernel, out_shape=[jax.ShapeDtypeStruct((2, 8, 128), F32),...  56.3 us
    pallas_call x1, Pallas kernels, shards(): pl.pallas_call(unpack_kernel, out_shape=[jax.ShapeDtypeStruct(shape, F32)...  2.16 us

profile of v5, /device:TPU:1, one launch (start us, length us, event | category | flops | bytes accessed | tf_op | source)
XLA Modules:
  0.0 59.1 jit_solution(13571136302611339484)
XLA Ops:
  0.6 56.3 %training_step.1 = (f32[2,8,128]{2,1,0:T(8,128)}, f32[32,16,128]{2,1,0:T(8,128)}) custom-call(bf16[6,32,32,128]{3,2,1,0:T(8,128)(2,1)} %fields_in.1, s32[32,32,128]{2,1,0:T(8,128)} %mask_in.1, f32[48,256]{1,0:T(8,128)} %constant.12.clone.ax_in, f32[768,128]{1,0:T(8,128)} %constant.13.clone.gy_in, f32[27,7,32]{2,1,0:T(8,128)} %bitcast.10, ...), custom_call_target="tpu_custom_call" | custom-call | tf_op jit(solution)/shard_map/training_step/pallas_call | solution.py:784
  56.9 2.2 %unpack_results.1 = (f32[4,4,16]{2,1,0:T(4,128)}, f32[4,4,16]{2,1,0:T(4,128)}, f32[27,7,32]{2,1,0:T(8,128)}, f32[27,32,32]{2,1,0:T(8,128)}, f32[27,32,32]{2,1,0:T(8,128)}, /*index=5*/f32[27,1,32]{2,1,0:T(1,128)}) custom-call(f32[2,8,128]{2,1,0:T(8,128)} %get-tuple-element.14.values, f32[32,16,128]{2,1,0:T(8,128)} %get-tuple-element.15.sums), custom_call_target="tpu_custom_call" | custom-call | tf_op jit(solution)/shard_map/unpack_results/pallas_call | solution.py:796
